TPU v7x, 32 devices: a whole 2x2x4 slice. The times are simulated.
32 devices in a mesh: ctx: 8 (over z, y), head: 4 (over x, core).
Axes of the slice: x: 2, y: 2, z: 4, core: 2. Of those that a mesh axis runs over, the one named last changes fastest.
Arguments:
- queries: bfloat16 [1024, 4096], P('ctx', 'head'), may hold values from -6 to 6
- keys: bfloat16 [1024, 4096], P('ctx', 'head'), may hold values from -0.52734375 to 0.52734375
- values: bfloat16 [1024, 4096], P('ctx', 'head'), may hold values from -6 to 6
- grad_out: bfloat16 [1024, 4096], P('ctx', 'head'), may hold values from -6 to 6
- token_kind: int32 [1024], P('ctx'), may hold values from 0 to 1
- level_table: int32 [2, 32, 8], P(None, 'head'), may hold values from 1 to 8
- head_scale: float32 [32], P('head'), may hold values from 0.5 to 4
- norm_gain: float32 [4096], P('head'), may hold values from 0.5 to 1.5
Outputs:
- attended: bfloat16 [1024, 4096], P('ctx', 'head')
- grad_queries: bfloat16 [1024, 4096], P('ctx', 'head')
- grad_keys: bfloat16 [1024, 4096], P('ctx', 'head')
- grad_values: bfloat16 [1024, 4096], P('ctx', 'head')
All inputs are finite; a program needn't handle non-finite values.
Results may differ from a plain program's by a relative error of at most 0.0057.
Values may be sent and summed in bfloat16 or wider, within the bound.
A program may use at most 64 MiB of HBM per device.

v0:
```python
import jax
import jax.numpy as jnp
from jax import lax
from jax.sharding import PartitionSpec as P

HEADS = 32
DH = 128
LEVELS = 8


EPSILON = 1e-06
HIGHEST_PRECISION = lax.Precision.HIGHEST


def partner_2(block, axis, apart):
    count = lax.axis_size(axis)
    route = []
    for low in range(count):
        high = low | 1 << apart
        if high != low and high < count:
            route += [(low, high), (high, low)]
    return lax.ppermute(block, axis, route)


def level_factors():
    return 0.25 * jnp.exp2(-0.5 * jnp.arange(LEVELS).astype(jnp.float32))


def shards(queries, keys, values, grad_out, token_kind, level_table, head_scale, norm_gain):
    token_count = queries.shape[0]
    local_heads = level_table.shape[1]
    head_width = queries.shape[1] // local_heads
    kind_count = level_table.shape[0]
    tree_depth = lax.axis_size("ctx").bit_length() - 1
    device_index = lax.axis_index("ctx")
    query_rows = queries.reshape(token_count, local_heads, head_width)
    key_rows = keys.reshape(token_count, local_heads, head_width)
    value_rows = values.reshape(token_count, local_heads, head_width)
    onehot = (token_kind[:, None] == jnp.arange(kind_count)[None, :]).astype(jnp.float32)
    weight_table = level_table.astype(jnp.float32) * level_factors()[None, None, :]
    level_weights = jnp.dot(
        onehot, weight_table.reshape(kind_count, -1), precision=HIGHEST_PRECISION
    )
    level_weights = level_weights.reshape(token_count, local_heads, -1)
    first_weights = level_weights[:, :, 0].T[:, :, None]
    causal = jnp.tril(jnp.ones((token_count, token_count), dtype=bool))
    scores = jnp.einsum("shd,uhd->hsu", query_rows, key_rows, preferred_element_type=jnp.float32)
    attn_probs = (jnp.where(causal[None], scores, 0.0) * first_weights).astype(jnp.bfloat16)
    readout = jnp.einsum("hsu,uhe->she", attn_probs, value_rows, preferred_element_type=jnp.float32)
    states = jnp.einsum("shd,she->hde", key_rows, value_rows, preferred_element_type=jnp.float32)
    upper_half = [(device_index >> height & 1).astype(jnp.float32) for height in range(tree_depth)]
    buckets = []

    def half_chain(half_sum):
        found = []
        for height in range(tree_depth):
            partner = partner_2(half_sum, "ctx", height)
            found.append((partner * upper_half[height]).astype(jnp.bfloat16))
            half_sum = half_sum + partner
        return found

    middle = local_heads // 2
    lower_found = half_chain(states[:middle])
    upper_found = half_chain(states[middle:])
    for height in range(tree_depth):
        buckets.append(jnp.concatenate([lower_found[height], upper_found[height]], axis=0))
    for height in range(tree_depth):
        readout = readout + level_weights[:, :, height + 1, None] * jnp.einsum(
            "shd,hde->she", query_rows, buckets[height], preferred_element_type=jnp.float32
        )
    scale = head_scale[None, :, None]
    gain = norm_gain.reshape(local_heads, head_width)[None]
    upstream = grad_out.reshape(token_count, local_heads, head_width).astype(jnp.float32)
    scaled = readout * scale
    square_sum, cross_sum = lax.psum(
        (jnp.sum(scaled * scaled, axis=(1, 2)), jnp.sum(gain * upstream * scaled, axis=(1, 2))),
        "head",
    )
    feature_count = HEADS * DH
    rms_value = jnp.sqrt(square_sum / feature_count + EPSILON)[:, None, None]
    attended = (scaled / rms_value * gain).astype(jnp.bfloat16).reshape(token_count, -1)
    cross_term = cross_sum[:, None, None]
    grad_scaled = gain * upstream / rms_value - scaled * (
        cross_term / (feature_count * rms_value**3)
    )
    grad_output = (grad_scaled * scale).astype(jnp.bfloat16)
    kind_mask = onehot.astype(jnp.bfloat16)
    grad_scores = jnp.einsum(
        "she,uhe->hsu", grad_output, value_rows, preferred_element_type=jnp.float32
    )
    grad_probs = (jnp.where(causal[None], grad_scores, 0.0) * first_weights).astype(jnp.bfloat16)
    query_local = jnp.einsum(
        "hsu,uhd->shd", grad_probs, key_rows, preferred_element_type=jnp.float32
    )
    key_local = jnp.einsum(
        "hsu,shd->uhd", grad_probs, query_rows, preferred_element_type=jnp.float32
    )
    value_local = jnp.einsum(
        "hsu,she->uhe", attn_probs, grad_output, preferred_element_type=jnp.float32
    )
    query_local, key_local, value_local = (query_local, key_local, value_local)
    level_query = jnp.zeros((token_count, local_heads, head_width), jnp.float32)
    for height in range(tree_depth):
        weight_now = level_weights[:, :, height + 1, None]
        level_query = level_query + weight_now * jnp.einsum(
            "she,hde->shd", grad_output, buckets[height], preferred_element_type=jnp.float32
        )
    masked_grad = grad_output[:, None, :, :] * kind_mask[:, :, None, None]
    kind_sums = jnp.einsum(
        "shd,skhe->khde", query_rows, masked_grad, preferred_element_type=jnp.float32
    )
    level_query, kind_sums = (level_query, kind_sums)
    group_sum = kind_sums
    accumulated = jnp.zeros_like(states)
    for height in range(tree_depth):
        partner = partner_2(group_sum, "ctx", height)
        level_weight = weight_table[:, :, height + 1]
        weighted = jnp.einsum("kh,khde->hde", level_weight, partner, precision=HIGHEST_PRECISION)
        accumulated = accumulated + (1.0 - upper_half[height]) * weighted
        group_sum = group_sum + partner
    state_grad = accumulated.astype(jnp.bfloat16)
    grad_query = query_local + level_query
    grad_key = key_local + jnp.einsum(
        "she,hde->shd", value_rows, state_grad, preferred_element_type=jnp.float32
    )
    grad_value = value_local + jnp.einsum(
        "shd,hde->she", key_rows, state_grad, preferred_element_type=jnp.float32
    )
    return (
        attended,
        grad_query.astype(jnp.bfloat16).reshape(token_count, -1),
        grad_key.astype(jnp.bfloat16).reshape(token_count, -1),
        grad_value.astype(jnp.bfloat16).reshape(token_count, -1),
    )


def solution(mesh):
    in_specs = (
        P("ctx", "head"),
        P("ctx", "head"),
        P("ctx", "head"),
        P("ctx", "head"),
        P("ctx"),
        P(None, "head", None),
        P("head"),
        P("head"),
    )
    out_specs = (P("ctx", "head"), P("ctx", "head"), P("ctx", "head"), P("ctx", "head"))
    return jax.shard_map(shards, mesh=mesh, in_specs=in_specs, out_specs=out_specs, check_vma=False)
```

profile of v0, /device:TPU:0, one launch (start us, length us, event | category | flops | bytes accessed | tf_op | source)
XLA Modules:
  0.0 164.4 jit_solution(9178713140820414310)
XLA Ops:
  0.6 1.0 copy.103
  2.2 3.0 %collective-permute-start = (f32[4,128,128]{2,1,0:T(8,128)S(1)}, f32[4,128,128]{2,1,0:T(8,128)S(1)}, u32[]{:S(2)}, u32[]{:S(2)}) collective-permute-start(f32[4,128,128]{2,1,0:T(8,128)S(1)} %get-tuple-element.23), channel_id=1, source_target_pairs={{0,4},{4,0},{8,12},{12,8},{16,20},{20,16},{24,28},{28,24},{1,5},{5... | collective-permute-start | bytes 786440 | tf_op jit(solution)/shard_map/ppermute | solution.py:22
  8.3 4.1 %collective-permute-done = f32[4,128,128]{2,1,0:T(8,128)S(1)} collective-permute-done((f32[4,128,128]{2,1,0:T(8,128)S(1)}, f32[4,128,128]{2,1,0:T(8,128)S(1)}, u32[]{:S(2)}, u32[]{:S(2)}) %collective-permute-start) | collective-permute-done | bytes 262176 | tf_op jit(solution)/shard_map/ppermute | solution.py:22
  12.4 4.8 %collective-permute-done.1 = f32[4,128,128]{2,1,0:T(8,128)S(1)} collective-permute-done((f32[4,128,128]{2,1,0:T(8,128)S(1)}, f32[4,128,128]{2,1,0:T(8,128)S(1)}, u32[]{:S(2)}, u32[]{:S(2)}) %collective-permute-start.1) | collective-permute-done | bytes 262176 | tf_op jit(solution)/shard_map/ppermute | solution.py:22
  17.3 1.9 %collective-permute-start.2 = (f32[4,128,128]{2,1,0:T(8,128)S(1)}, f32[4,128,128]{2,1,0:T(8,128)}, u32[]{:S(2)}, u32[]{:S(2)}) collective-permute-start(f32[4,128,128]{2,1,0:T(8,128)S(1)} %get-tuple-element.21), channel_id=1, source_target_pairs={{0,8},{8,0},{4,12},{12,4},{16,24},{24,16},{20,28},{28,20},{1,9},{9... | collective-permute-start | bytes 786440 | tf_op jit(solution)/shard_map/ppermute | solution.py:22
  20.4 6.3 %collective-permute-done.2 = f32[4,128,128]{2,1,0:T(8,128)} collective-permute-done((f32[4,128,128]{2,1,0:T(8,128)S(1)}, f32[4,128,128]{2,1,0:T(8,128)}, u32[]{:S(2)}, u32[]{:S(2)}) %collective-permute-start.2) | collective-permute-done | bytes 262176 | tf_op jit(solution)/shard_map/ppermute | solution.py:22
  26.7 1.0 multiply_convert_fusion.5
  27.7 2.9 %collective-permute-start.4 = (f32[4,128,128]{2,1,0:T(8,128)S(1)}, f32[4,128,128]{2,1,0:T(8,128)S(1)}, u32[]{:S(2)}, u32[]{:S(2)}) collective-permute-start(f32[4,128,128]{2,1,0:T(8,128)S(1)} %get-tuple-element.28), channel_id=1, source_target_pairs={{0,16},{16,0},{4,20},{20,4},{8,24},{24,8},{12,28},{28,12},{1,17},{... | collective-permute-start | bytes 786440 | tf_op jit(solution)/shard_map/ppermute | solution.py:22
  30.5 3.8 %collective-permute-done.3 = f32[4,128,128]{2,1,0:T(8,128)S(1)} collective-permute-done((f32[4,128,128]{2,1,0:T(8,128)S(1)}, f32[4,128,128]{2,1,0:T(8,128)S(1)}, u32[]{:S(2)}, u32[]{:S(2)}) %collective-permute-start.3) | collective-permute-done | bytes 262176 | tf_op jit(solution)/shard_map/ppermute | solution.py:22
  35.4 11.4 %collective-permute-done.4 = f32[4,128,128]{2,1,0:T(8,128)S(1)} collective-permute-done((f32[4,128,128]{2,1,0:T(8,128)S(1)}, f32[4,128,128]{2,1,0:T(8,128)S(1)}, u32[]{:S(2)}, u32[]{:S(2)}) %collective-permute-start.4) | collective-permute-done | bytes 262176 | tf_op jit(solution)/shard_map/ppermute | solution.py:22
  46.8 4.1 %collective-permute-done.5 = f32[4,128,128]{2,1,0:T(8,128)S(1)} collective-permute-done((f32[4,128,128]{2,1,0:T(8,128)S(1)}, f32[4,128,128]{2,1,0:T(8,128)S(1)}, u32[]{:S(2)}, u32[]{:S(2)}) %collective-permute-start.5) | collective-permute-done | bytes 262176 | tf_op jit(solution)/shard_map/ppermute | solution.py:22
  52.9 5.7 %all-reduce = (f32[128]{0:T(128)S(1)}, f32[128]{0:T(128)S(1)}) all-reduce(f32[128]{0:T(128)S(1)} %get-tuple-element.13, f32[128]{0:T(128)S(1)} %get-tuple-element.12), channel_id=1, replica_groups=mesh['ctx'=8,'head'=4] {'head'}, use_global_device_ids=true, to_apply=%region_1.2 | all-reduce | flops 256 | bytes 2048 | tf_op jit(solution)/shard_map/psum | solution.py:75
  59.3 0.9 multiply_convert_fusion
  61.2 1.7 %collective-permute-start.6 = (f32[2,8,128,128]{2,3,0,1:T(8,128)S(1)}, f32[2,8,128,128]{2,3,0,1:T(8,128)S(1)}, u32[]{:S(2)}, u32[]{:S(2)}) collective-permute-start(f32[2,8,128,128]{2,3,0,1:T(8,128)S(1)} %convolution_bitcast_fusion), channel_id=1, source_target_pairs={{0,4},{4,0},{8,12},{12,8},{16,20},{20,16},{24,28},{28,24},{1,5},{5... | collective-permute-start | bytes 3145736 | tf_op jit(solution)/shard_map/ppermute | solution.py:22
  62.9 23.3 %collective-permute-done.6 = f32[2,8,128,128]{2,3,0,1:T(8,128)S(1)} collective-permute-done((f32[2,8,128,128]{2,3,0,1:T(8,128)S(1)}, f32[2,8,128,128]{2,3,0,1:T(8,128)S(1)}, u32[]{:S(2)}, u32[]{:S(2)}) %collective-permute-start.6) | collective-permute-done | bytes 1048608 | tf_op jit(solution)/shard_map/ppermute | solution.py:22
  90.6 1.8 %copy.64 = bf16[128,1024]{1,0:T(8,128)(2,1)} copy(bf16[128,1024]{0,1:T(8,128)(2,1)} %bitcast.148) | data formatting | bytes 524288
  92.4 1.2 fusion.14
  94.9 15.6 %collective-permute-done.7 = f32[2,8,128,128]{2,3,0,1:T(8,128)} collective-permute-done((f32[2,8,128,128]{2,3,0,1:T(8,128)S(1)}, f32[2,8,128,128]{2,3,0,1:T(8,128)}, u32[]{:S(2)}, u32[]{:S(2)}) %collective-permute-start.7) | collective-permute-done | bytes 1048608 | tf_op jit(solution)/shard_map/ppermute | solution.py:22
  110.6 2.3 %add.73 = f32[2,8,128,128]{2,3,0,1:T(8,128)} add(f32[2,8,128,128]{2,3,0,1:T(8,128)S(1)} %add.71, f32[2,8,128,128]{2,3,0,1:T(8,128)} %collective-permute-done.7) | non-fusion elementwise | flops 262144 | bytes 3145728 | tf_op jit(solution)/shard_map/add | solution.py:120
  112.9 1.4 collective-permute-start.8
  117.8 1.4 multiply_reduce_fusion.1
  119.3 40.4 %collective-permute-done.8 = f32[2,8,128,128]{2,3,0,1:T(8,128)} collective-permute-done((f32[2,8,128,128]{2,3,0,1:T(8,128)}, f32[2,8,128,128]{2,3,0,1:T(8,128)}, u32[]{:S(2)}, u32[]{:S(2)}) %collective-permute-start.8) | collective-permute-done | bytes 1048608 | tf_op jit(solution)/shard_map/ppermute | solution.py:22
  159.7 1.4 multiply_reduce_fusion
  162.7 0.9 copy.66
  (108 shorter events, 21.1 us)
Async XLA Ops:
  0.6 1.3 copy-start
  2.1 3.2 %copy-start.21 = (s32[2,8,8]{2,1,0:T(8,128)S(1)}, s32[2,8,8]{2,1,0:T(8,128)}, u32[]{:S(2)}) copy-start(s32[2,8,8]{2,1,0:T(8,128)} %param.13) | copy-start | bytes 1540
  2.2 4.8 %copy-start.12 = (bf16[128,1024]{1,0:T(8,128)(2,1)S(1)}, bf16[128,1024]{1,0:T(8,128)(2,1)}, u32[]{:S(2)}) copy-start(bf16[128,1024]{1,0:T(8,128)(2,1)} %param.8) | copy-start | bytes 786436
  2.2 10.2 %collective-permute-start = (f32[4,128,128]{2,1,0:T(8,128)S(1)}, f32[4,128,128]{2,1,0:T(8,128)S(1)}, u32[]{:S(2)}, u32[]{:S(2)}) collective-permute-start(f32[4,128,128]{2,1,0:T(8,128)S(1)} %get-tuple-element.23), channel_id=1, source_target_pairs={{0,4},{4,0},{8,12},{12,8},{16,20},{20,16},{24,28},{28,24},{1,5},{5... | collective-permute-start | bytes 786440 | tf_op jit(solution)/shard_map/ppermute | solution.py:22
  5.2 11.9 %collective-permute-start.1 = (f32[4,128,128]{2,1,0:T(8,128)S(1)}, f32[4,128,128]{2,1,0:T(8,128)S(1)}, u32[]{:S(2)}, u32[]{:S(2)}) collective-permute-start(f32[4,128,128]{2,1,0:T(8,128)S(1)} %get-tuple-element.24), channel_id=1, source_target_pairs={{0,4},{4,0},{8,12},{12,8},{16,20},{20,16},{24,28},{28,24},{1,5},{5... | collective-permute-start | bytes 786440 | tf_op jit(solution)/shard_map/ppermute | solution.py:22
  7.0 1.0 copy-start.5
  8.3 43.6 %copy-start.7 = (bf16[8,128,128]{2,1,0:T(8,128)(2,1)}, bf16[8,128,128]{2,1,0:T(8,128)(2,1)S(1)}, u32[]{:S(2)}) copy-start(bf16[8,128,128]{2,1,0:T(8,128)(2,1)S(1)} %fusion.16) | copy-start | bytes 786436
  8.3 11.3 %copy-start.11 = (bf16[128,1024]{1,0:T(8,128)(2,1)S(1)}, bf16[128,1024]{1,0:T(8,128)(2,1)}, u32[]{:S(2)}) copy-start(bf16[128,1024]{1,0:T(8,128)(2,1)} %param.11) | copy-start | bytes 786436
  17.3 9.4 %collective-permute-start.2 = (f32[4,128,128]{2,1,0:T(8,128)S(1)}, f32[4,128,128]{2,1,0:T(8,128)}, u32[]{:S(2)}, u32[]{:S(2)}) collective-permute-start(f32[4,128,128]{2,1,0:T(8,128)S(1)} %get-tuple-element.21), channel_id=1, source_target_pairs={{0,8},{8,0},{4,12},{12,4},{16,24},{24,16},{20,28},{28,20},{1,9},{9... | collective-permute-start | bytes 786440 | tf_op jit(solution)/shard_map/ppermute | solution.py:22
  19.8 14.5 %collective-permute-start.3 = (f32[4,128,128]{2,1,0:T(8,128)S(1)}, f32[4,128,128]{2,1,0:T(8,128)S(1)}, u32[]{:S(2)}, u32[]{:S(2)}) collective-permute-start(f32[4,128,128]{2,1,0:T(8,128)S(1)} %get-tuple-element.22), channel_id=1, source_target_pairs={{0,8},{8,0},{4,12},{12,4},{16,24},{24,16},{20,28},{28,20},{1,9},{9... | collective-permute-start | bytes 786440 | tf_op jit(solution)/shard_map/ppermute | solution.py:22
  27.7 19.1 %collective-permute-start.4 = (f32[4,128,128]{2,1,0:T(8,128)S(1)}, f32[4,128,128]{2,1,0:T(8,128)S(1)}, u32[]{:S(2)}, u32[]{:S(2)}) collective-permute-start(f32[4,128,128]{2,1,0:T(8,128)S(1)} %get-tuple-element.28), channel_id=1, source_target_pairs={{0,16},{16,0},{4,20},{20,4},{8,24},{24,8},{12,28},{28,12},{1,17},{... | collective-permute-start | bytes 786440 | tf_op jit(solution)/shard_map/ppermute | solution.py:22
  34.3 1.1 copy-start.1
  34.3 16.6 %collective-permute-start.5 = (f32[4,128,128]{2,1,0:T(8,128)S(1)}, f32[4,128,128]{2,1,0:T(8,128)S(1)}, u32[]{:S(2)}, u32[]{:S(2)}) collective-permute-start(f32[4,128,128]{2,1,0:T(8,128)S(1)} %get-tuple-element.30), channel_id=1, source_target_pairs={{0,16},{16,0},{4,20},{20,4},{8,24},{24,8},{12,28},{28,12},{1,17},{... | collective-permute-start | bytes 786440 | tf_op jit(solution)/shard_map/ppermute | solution.py:22
  46.8 5.0 %copy-start.3 = (bf16[4,128,128]{2,1,0:T(8,128)(2,1)}, bf16[4,128,128]{2,1,0:T(8,128)(2,1)S(1)}, u32[]{:S(2)}) copy-start(bf16[4,128,128]{2,1,0:T(8,128)(2,1)S(1)} %multiply_convert_fusion.3) | copy-start | bytes 393220
  50.9 1.0 copy-start.4
  61.2 25.0 %collective-permute-start.6 = (f32[2,8,128,128]{2,3,0,1:T(8,128)S(1)}, f32[2,8,128,128]{2,3,0,1:T(8,128)S(1)}, u32[]{:S(2)}, u32[]{:S(2)}) collective-permute-start(f32[2,8,128,128]{2,3,0,1:T(8,128)S(1)} %convolution_bitcast_fusion), channel_id=1, source_target_pairs={{0,4},{4,0},{8,12},{12,8},{16,20},{20,16},{24,28},{28,24},{1,5},{5... | collective-permute-start | bytes 3145736 | tf_op jit(solution)/shard_map/ppermute | solution.py:22
  86.3 24.2 %collective-permute-start.7 = (f32[2,8,128,128]{2,3,0,1:T(8,128)S(1)}, f32[2,8,128,128]{2,3,0,1:T(8,128)}, u32[]{:S(2)}, u32[]{:S(2)}) collective-permute-start(f32[2,8,128,128]{2,3,0,1:T(8,128)S(1)} %add.71), channel_id=1, source_target_pairs={{0,8},{8,0},{4,12},{12,4},{16,24},{24,16},{20,28},{28,20},{1,9},{9... | collective-permute-start | bytes 3145736 | tf_op jit(solution)/shard_map/ppermute | solution.py:22
  90.6 1.8 %copy-start.14 = (f32[128,8,1]{0,2,1:T(1,128)S(1)}, f32[128,8,1]{0,2,1:T(1,128)}, u32[]{:S(2)}) copy-start(f32[128,8,1]{0,2,1:T(1,128)} %get-tuple-element.32) | copy-start | bytes 12292
  92.4 1.2 copy-start.2
  94.7 19.6 %copy-start.9 = (bf16[8,128,128]{2,1,0:T(8,128)(2,1)}, bf16[8,128,128]{2,1,0:T(8,128)(2,1)S(1)}, u32[]{:S(2)}) copy-start(bf16[8,128,128]{2,1,0:T(8,128)(2,1)S(1)} %fusion.17) | copy-start | bytes 786436
  112.9 46.8 %collective-permute-start.8 = (f32[2,8,128,128]{2,3,0,1:T(8,128)}, f32[2,8,128,128]{2,3,0,1:T(8,128)}, u32[]{:S(2)}, u32[]{:S(2)}) collective-permute-start(f32[2,8,128,128]{2,3,0,1:T(8,128)} %add.73), channel_id=1, source_target_pairs={{0,16},{16,0},{4,20},{20,4},{8,24},{24,8},{12,28},{28,12},{1,17},{... | collective-permute-start | bytes 3145736 | tf_op jit(solution)/shard_map/ppermute | solution.py:22
  114.6 1.0 copy-start.10
  115.5 0.9 copy-start.8
  161.1 1.0 copy-start.6
  (16 other events, 10.7 us)
where the time goes:
time: 165 us; the launch traced here: 164 us
  waiting for transfers between devices  114 us (69%)
  local copies, waits for them, and re-layouts  18.1 us (11%)
  starting transfers between devices  12.1 us (7%)
  other arithmetic  8.15 us (5%)
  blocking collectives  5.66 us (3%)
  matrix products  5.6 us (3%)
    ppermute x9, waiting for transfers between devices, partner_2(): return lax.ppermute(block, axis, route)  114 us
    unnamed x71, local copies, waits for them, and re-layouts  16 us
    ppermute x9, starting transfers between devices, partner_2(): return lax.ppermute(block, axis, route)  12.1 us
    psum x1, blocking collectives, shards(): lax.psum((jnp.sum(scaled * scaled, axis=(1, 2)), jnp.sum(gain * upstream...  5.66 us
  transfers between devices with their start and end apart: 9, of which 9 were waited for; matrix products, arithmetic and copies ran while one was open for 8% of the time, Pallas kernels for 0%

commit v1 on v0

v1 whole, which is shorter than its diff:
```python
import functools

import jax
import jax.numpy as jnp
from jax import lax
from jax.experimental import pallas as pl
from jax.experimental.pallas import tpu as pltpu
from jax.sharding import PartitionSpec as P

EPSILON = 1e-06
CHUNK = 2
F32 = jnp.float32
BF16 = jnp.bfloat16


def factor(level):
    return 0.25 * 2.0 ** (-0.5 * level)


def dot(left, right, contract):
    return lax.dot_general(left, right, (contract, ((), ())), preferred_element_type=F32)


NN = ((1,), (0,))
NT = ((1,), (1,))
TN = ((0,), (0,))


def kernel(
    ctx_count, head_count,
    q_hbm, k_hbm, v_hbm, dy_hbm, kind_ref, table_ref, scale_ref, gain_ref,
    att_ref, gq_ref, gk_ref, gv_ref,
    q_ref, k_ref, v_ref, dy_ref, kind_col, inv_col, coef_col,
    states, probs, query_t, readout, grad_out_ref, kind_sums, grad_states, key_acc, value_acc,
    fwd_send, fwd_recv, bwd_send, bwd_recv, stat_send, stat_recv,
    load_sem, fwd_ssem, fwd_rsem, bwd_ssem, bwd_rsem, stat_ssem, stat_rsem,
):
    tokens, width = q_ref.shape
    heads, size, _ = states.shape
    kinds = table_ref.shape[0]
    depth = ctx_count.bit_length() - 1
    chunks = heads // CHUNK
    c = lax.axis_index("ctx")
    me = lax.axis_index("head")
    partner = [c ^ (1 << b) for b in range(depth)]
    bit = [(c >> b) & 1 for b in range(depth)]
    upper = [bit[b] == 1 for b in range(depth)]
    need = [(c >> (b + 1)) != (ctx_count >> (b + 1)) - 1 for b in range(depth)]
    fwd_sends = [jnp.logical_or(bit[b] == 0, need[b]) for b in range(depth)]
    fwd_recvs = [jnp.logical_or(bit[b] == 1, need[b]) for b in range(depth)]
    bwd_sends = fwd_recvs
    bwd_recvs = fwd_sends

    loads = [
        pltpu.make_async_copy(src, dst, load_sem.at[i])
        for i, (src, dst) in enumerate(
            ((k_hbm, k_ref), (v_hbm, v_ref), (q_hbm, q_ref), (dy_hbm, dy_ref))
        )
    ]
    for load in loads:
        load.start()
    barrier = pltpu.get_barrier_semaphore()
    for b in range(depth):
        pl.semaphore_signal(barrier, inc=1, device_id={"ctx": partner[b]}, device_id_type=pl.DeviceIdType.MESH)
    for d in range(1, head_count):
        pl.semaphore_signal(
            barrier, inc=1, device_id={"head": lax.rem(me + d, head_count)},
            device_id_type=pl.DeviceIdType.MESH,
        )

    def cols(h):
        return pl.ds(h * size, size)

    def chunk_heads(j):
        return range(j * CHUNK, (j + 1) * CHUNK)

    def exchange(send, recv, ssem, rsem, b, j):
        part = pl.ds(j * CHUNK, CHUNK)
        return pltpu.make_async_remote_copy(
            src_ref=send.at[b, part], dst_ref=recv.at[b, part],
            send_sem=ssem.at[b, j], recv_sem=rsem.at[b, j],
            device_id={"ctx": partner[b]}, device_id_type=pl.DeviceIdType.MESH,
        )

    fwd = functools.partial(exchange, fwd_send, fwd_recv, fwd_ssem, fwd_rsem)
    bwd = functools.partial(exchange, bwd_send, bwd_recv, bwd_ssem, bwd_rsem)

    def weight(kind, h, level):
        return table_ref[kind, h, level].astype(F32) * factor(level)

    def token_weights(h, level):
        out = jnp.full((tokens, size), weight(0, h, level), F32)
        for kind in range(1, kinds):
            out = jnp.where(kind_col[...] == kind, weight(kind, h, level), out)
        return out

    def causal():
        row = lax.broadcasted_iota(jnp.int32, (tokens, tokens), 0)
        col = lax.broadcasted_iota(jnp.int32, (tokens, tokens), 1)
        return col <= row

    loads[0].wait()
    loads[1].wait()
    for j in range(chunks):
        for h in chunk_heads(j):
            state = dot(k_ref[:, cols(h)], v_ref[:, cols(h)], TN)
            states[h] = state
            fwd_send[0, h] = state.astype(BF16)
        if j == 0:
            pl.semaphore_wait(barrier, depth + head_count - 1)

        @pl.when(fwd_sends[0])
        def _():
            fwd(0, j).start()

    loads[2].wait()
    loads[3].wait()
    kind_col[...] = jnp.transpose(
        jnp.broadcast_to(kind_ref[...].astype(F32), (size, tokens))
    )

    def local_forward(j):
        for h in chunk_heads(j):
            q = q_ref[:, cols(h)]
            scores = dot(q, k_ref[:, cols(h)], NT)
            attn = (jnp.where(causal(), scores, 0.0) * token_weights(h, 0)).astype(BF16)
            probs[h] = attn
            readout[h] = dot(attn, v_ref[:, cols(h)], NN)
            query_t[h] = jnp.transpose(q)

    def receive_forward(b, j):
        @pl.when(fwd_recvs[b])
        def _():
            fwd(b, j).wait_recv()
            if b + 1 < depth:
                for h in chunk_heads(j):
                    total = states[h] + fwd_recv[b, h].astype(F32)
                    states[h] = total
                    fwd_send[b + 1, h] = total.astype(BF16)

        if b + 1 < depth:

            @pl.when(fwd_sends[b + 1])
            def _():
                fwd(b + 1, j).start()

        @pl.when(upper[b])
        def _():
            for h in chunk_heads(j):
                level = dot(q_ref[:, cols(h)], fwd_recv[b, h], NN)
                readout[h] += token_weights(h, b + 1) * level

    squares = jnp.zeros((tokens, size), F32)
    crosses = jnp.zeros((tokens, size), F32)
    for step in range(chunks + depth - 1):
        if step < chunks:
            local_forward(step)
        for b in reversed(range(depth)):
            j = step - b
            if 0 <= j < chunks:
                receive_forward(b, j)
        j = step - depth + 1
        if 0 <= j < chunks:
            for h in chunk_heads(j):
                z = readout[h] * scale_ref[h]
                readout[h] = z
                squares += z * z
                crosses += gain_ref[:, cols(h)] * dy_ref[:, cols(h)].astype(F32) * z

    stat_send[0:1, :] = jnp.sum(jnp.transpose(squares), axis=0, keepdims=True)
    stat_send[1:2, :] = jnp.sum(jnp.transpose(crosses), axis=0, keepdims=True)
    stat_copies = [
        pltpu.make_async_remote_copy(
            src_ref=stat_send, dst_ref=stat_recv.at[d - 1],
            send_sem=stat_ssem.at[d - 1], recv_sem=stat_rsem.at[d - 1],
            device_id={"head": lax.rem(me + d, head_count)},
            device_id_type=pl.DeviceIdType.MESH,
        )
        for d in range(1, head_count)
    ]
    for copy in stat_copies:
        copy.start()
    square_row = stat_send[0:1, :]
    cross_row = stat_send[1:2, :]
    for d, copy in enumerate(stat_copies):
        copy.wait_recv()
        square_row += stat_recv[d, 0:1, :]
        cross_row += stat_recv[d, 1:2, :]
    features = width * head_count
    rms = jnp.sqrt(square_row / features + EPSILON)
    coef = cross_row / (features * rms * rms * rms)
    inv_col[...] = jnp.transpose(jnp.broadcast_to(1.0 / rms, (size, tokens)))
    coef_col[...] = jnp.transpose(jnp.broadcast_to(coef, (size, tokens)))

    def message(b, h, flag):
        total = None
        for kind in range(kinds):
            term = (weight(kind, h, b + 1) * flag) * kind_sums[h, :, pl.ds(kind * size, size)]
            total = term if total is None else total + term
        return total

    for j in range(chunks):
        for h in chunk_heads(j):
            gain = gain_ref[:, cols(h)]
            z = readout[h]
            att_ref[:, cols(h)] = (z * inv_col[...] * gain).astype(BF16)
            grad = gain * dy_ref[:, cols(h)].astype(F32) * inv_col[...] - z * coef_col[...]
            grad = (grad * scale_ref[h]).astype(BF16)
            grad_out_ref[h] = grad
            masked = jnp.concatenate(
                [jnp.where(kind_col[...] == kind, grad.astype(F32), 0.0).astype(BF16) for kind in range(kinds)],
                axis=1,
            )
            kind_sums[h] = dot(query_t[h], masked, NN)
            grad_states[h] = jnp.zeros((size, size), F32)

        @pl.when(bwd_sends[depth - 1])
        def _():
            for h in chunk_heads(j):
                bwd_send[depth - 1, h] = message(depth - 1, h, 1.0).astype(BF16)
            bwd(depth - 1, j).start()

    def local_backward(j):
        for h in chunk_heads(j):
            grad = grad_out_ref[h]
            scores = dot(grad, v_ref[:, cols(h)], NT)
            dprobs = (jnp.where(causal(), scores, 0.0) * token_weights(h, 0)).astype(BF16)
            key_acc[h] = dot(dprobs, q_ref[:, cols(h)], TN)
            value_acc[h] = dot(probs[h], grad, TN)
            readout[h] = dot(dprobs, k_ref[:, cols(h)], NN)
        for b in range(depth):

            @pl.when(upper[b])
            def _():
                for h in chunk_heads(j):
                    level = dot(grad_out_ref[h], fwd_recv[b, h], NT)
                    readout[h] += token_weights(h, b + 1) * level

        for h in chunk_heads(j):
            gq_ref[:, cols(h)] = readout[h].astype(BF16)

    def receive_backward(b, j):
        @pl.when(bwd_recvs[b])
        def _():
            bwd(b, j).wait_recv()
            for h in chunk_heads(j):
                grad_states[h] += bwd_recv[b, h].astype(F32)

        if b > 0:

            @pl.when(bwd_sends[b - 1])
            def _():
                flag = bit[b - 1].astype(F32)
                for h in chunk_heads(j):
                    bwd_send[b - 1, h] = (grad_states[h] + message(b - 1, h, flag)).astype(BF16)
                bwd(b - 1, j).start()

        else:
            for h in chunk_heads(j):
                state = grad_states[h].astype(BF16)
                gk_ref[:, cols(h)] = (key_acc[h] + dot(v_ref[:, cols(h)], state, NT)).astype(BF16)
                gv_ref[:, cols(h)] = (value_acc[h] + dot(k_ref[:, cols(h)], state, NN)).astype(BF16)

    for step in range(chunks + depth - 1):
        if step < chunks:
            local_backward(step)
        for b in range(depth):
            j = step - (depth - 1 - b)
            if 0 <= j < chunks:
                receive_backward(b, j)

    for copy in stat_copies:
        copy.wait_send()
    for b in range(depth):

        @pl.when(fwd_sends[b])
        def _():
            for j in range(chunks):
                fwd(b, j).wait_send()

        @pl.when(bwd_sends[b])
        def _():
            for j in range(chunks):
                bwd(b, j).wait_send()


def solution(mesh):
    ctx_count, head_count = mesh.shape["ctx"], mesh.shape["head"]
    depth = ctx_count.bit_length() - 1

    def shards(queries, keys, values, grad_out, token_kind, level_table, head_scale, norm_gain):
        tokens, width = queries.shape
        kinds, heads, _ = level_table.shape
        size = width // heads
        chunks = heads // CHUNK
        anywhere = pl.BlockSpec(memory_space=pl.ANY)
        vmem = pl.BlockSpec(memory_space=pltpu.VMEM)
        smem = pl.BlockSpec(memory_space=pltpu.SMEM)
        block = jax.ShapeDtypeStruct((tokens, width), BF16)
        square = (heads, size, size)
        return pl.pallas_call(
            functools.partial(kernel, ctx_count, head_count),
            out_shape=(block,) * 4,
            in_specs=[anywhere] * 4 + [vmem, smem, smem, vmem],
            out_specs=(vmem,) * 4,
            scratch_shapes=[pltpu.VMEM((tokens, width), BF16)] * 4
            + [pltpu.VMEM((tokens, size), F32)] * 3
            + [
                pltpu.VMEM(square, F32),
                pltpu.VMEM((heads, tokens, tokens), BF16),
                pltpu.VMEM((heads, size, tokens), BF16),
                pltpu.VMEM((heads, tokens, size), F32),
                pltpu.VMEM((heads, tokens, size), BF16),
                pltpu.VMEM((heads, size, kinds * size), F32),
                pltpu.VMEM(square, F32),
                pltpu.VMEM((heads, tokens, size), F32),
                pltpu.VMEM((heads, tokens, size), F32),
            ]
            + [pltpu.VMEM((depth,) + square, BF16)] * 4
            + [
                pltpu.VMEM((8, tokens), F32),
                pltpu.VMEM((head_count - 1, 8, tokens), F32),
                pltpu.SemaphoreType.DMA((4,)),
            ]
            + [pltpu.SemaphoreType.DMA((depth, chunks))] * 4
            + [pltpu.SemaphoreType.DMA((head_count - 1,))] * 2,
            compiler_params=pltpu.CompilerParams(
                collective_id=0, has_side_effects=True, vmem_limit_bytes=40 * 1024 * 1024
            ),
            cost_estimate=pl.CostEstimate(
                flops=36 * heads * tokens * size * size, bytes_accessed=16 * tokens * width, transcendentals=0
            ),
        )(
            queries, keys, values, grad_out,
            token_kind.reshape(1, tokens), level_table, head_scale, norm_gain.reshape(1, width),
        )

    in_specs = (
        P("ctx", "head"),
        P("ctx", "head"),
        P("ctx", "head"),
        P("ctx", "head"),
        P("ctx"),
        P(None, "head", None),
        P("head"),
        P("head"),
    )
    return jax.shard_map(
        shards, mesh=mesh, in_specs=in_specs, out_specs=(P("ctx", "head"),) * 4, check_vma=False
    )
```

time: 165 us -> 69.7 us (0.42)
  waiting for transfers between devices: 114 us -> 0 us
  Pallas kernels: 0 us -> 60.1 us
  starting transfers between devices: 12.1 us -> 0 us
  local copies, waits for them, and re-layouts: 18.1 us -> 8.65 us
  other arithmetic: 8.15 us -> 0 us
  blocking collectives: 5.66 us -> 0 us
  matrix products: 5.6 us -> 0 us
    ppermute x9 -> x0, waiting for transfers between devices: 114 us -> none  [partner_2(): return lax.ppermute(block, axis, route)]
    pallas_call x0 -> x1, Pallas kernels: none -> 60.1 us  [shards(): pl.pallas_call(functools.partial(kernel, ctx_count, head_count), out_shap...]
    ppermute x9 -> x0, starting transfers between devices: 12.1 us -> none  [partner_2(): return lax.ppermute(block, axis, route)]
    unnamed x71 -> x20, local copies, waits for them, and re-layouts: 16 us -> 8.65 us
    psum x1 -> x0, blocking collectives: 5.66 us -> none  [shards(): lax.psum((jnp.sum(scaled * scaled, axis=(1, 2)), jnp.sum(gain * upstream...]
    dot_general x17 -> x0, matrix products: 5.6 us -> none  [the longest x3 1.66 us: shards(): jnp.einsum('she,hde->shd', grad_output, buckets[height], preferred_elemen...]
    dot_general x3 -> x0, other arithmetic: 2.95 us -> none  [shards(): jnp.einsum('kh,khde->hde', level_weight, partner, precision=HIGHEST_PRECI...]
    convert_element_type x7 -> x0, other arithmetic: 2.65 us -> none  [the longest x4 1.07 us: half_chain(): found.append((partner * upper_half[height]).astype(jnp.bfloat16))]
  transfers between devices with their start and end apart: 9 -> 0, of which waited for: 9 -> 0; matrix products, arithmetic and copies ran while one was open for 8% -> 0% of each run, Pallas kernels for 0% -> 0%
where the time goes in v1:
time: 69.7 us; the launch traced here: 69.4 us
  Pallas kernels  60.1 us (86%)
  local copies, waits for them, and re-layouts  8.65 us (12%)
    pallas_call x1, Pallas kernels, shards(): pl.pallas_call(functools.partial(kernel, ctx_count, head_count), out_shap...  60.1 us
    unnamed x20, local copies, waits for them, and re-layouts  8.65 us

profile of v1, /device:TPU:0, one launch (start us, length us, event | category | flops | bytes accessed | tf_op | source)
XLA Modules:
  0.0 69.4 jit_solution(10445901254640331339)
XLA Ops:
  0.6 0.0 copy-start.6
  0.6 0.0 copy-start.7
  0.7 0.6 copy-done.6
  1.3 0.0 copy-done.7
  1.3 0.0 copy-start
  1.3 0.9 %copy-done = bf16[128,1024]{1,0:T(8,128)(2,1)S(1)} copy-done((bf16[128,1024]{1,0:T(8,128)(2,1)S(1)}, bf16[128,1024]{1,0:T(8,128)(2,1)}, u32[]{:S(2)}) %copy-start) | copy-done | bytes 262168
  2.3 0.0 copy-start.1
  2.3 0.9 %copy-done.1 = bf16[128,1024]{1,0:T(8,128)(2,1)S(1)} copy-done((bf16[128,1024]{1,0:T(8,128)(2,1)S(1)}, bf16[128,1024]{1,0:T(8,128)(2,1)}, u32[]{:S(2)}) %copy-start.1) | copy-done | bytes 262168
  3.2 0.0 copy-start.2
  3.2 0.9 %copy-done.2 = bf16[128,1024]{1,0:T(8,128)(2,1)S(1)} copy-done((bf16[128,1024]{1,0:T(8,128)(2,1)S(1)}, bf16[128,1024]{1,0:T(8,128)(2,1)}, u32[]{:S(2)}) %copy-start.2) | copy-done | bytes 262168
  4.2 0.0 copy-start.3
  4.2 0.9 %copy-done.3 = bf16[128,1024]{1,0:T(8,128)(2,1)S(1)} copy-done((bf16[128,1024]{1,0:T(8,128)(2,1)S(1)}, bf16[128,1024]{1,0:T(8,128)(2,1)}, u32[]{:S(2)}) %copy-start.3) | copy-done | bytes 262168
  5.1 0.0 copy-start.4
  5.1 0.7 %copy-done.4 = s32[2,8,8]{2,1,0:T(8,128)S(1)} copy-done((s32[2,8,8]{2,1,0:T(8,128)S(1)}, s32[2,8,8]{2,1,0:T(8,128)}, u32[]{:S(2)}) %copy-start.4) | copy-done | bytes 536
  5.8 0.0 copy-start.5
  5.8 0.7 copy-done.5
  6.5 60.1 %shard_map.111 = (bf16[128,1024]{1,0:T(8,128)(2,1)S(1)}, bf16[128,1024]{1,0:T(8,128)(2,1)S(1)}, bf16[128,1024]{1,0:T(8,128)(2,1)S(1)}, bf16[128,1024]{1,0:T(8,128)(2,1)S(1)}) custom-call(bf16[128,1024]{1,0:T(8,128)(2,1)S(1)} %copy-done, bf16[128,1024]{1,0:T(8,128)(2,1)S(1)} %copy-done.1, bf16[128,1024]{1,0:T(8,128)(2,1)S(1)} %copy-done.2, ...), custom_call_target="tpu_custom_call" | custom-call | flops 603979776 | bytes 2097152 | tf_op jit(solution)/shard_map/pallas_call | solution.py:301
  66.6 0.7 %copy.16 = bf16[128,1024]{1,0:T(8,128)(2,1)} copy(bf16[128,1024]{1,0:T(8,128)(2,1)S(1)} %get-tuple-element.8) | data formatting | bytes 524288
  67.3 0.7 %copy.17 = bf16[128,1024]{1,0:T(8,128)(2,1)} copy(bf16[128,1024]{1,0:T(8,128)(2,1)S(1)} %get-tuple-element.9) | data formatting | bytes 524288
  68.0 0.7 %copy.18 = bf16[128,1024]{1,0:T(8,128)(2,1)} copy(bf16[128,1024]{1,0:T(8,128)(2,1)S(1)} %get-tuple-element.10) | data formatting | bytes 524288
  68.7 0.7 %copy.19 = bf16[128,1024]{1,0:T(8,128)(2,1)} copy(bf16[128,1024]{1,0:T(8,128)(2,1)S(1)} %get-tuple-element.11) | data formatting | bytes 524288
Async XLA Ops:
  0.6 0.7 copy-start.6
  0.6 0.7 copy-start.7
  1.3 0.9 %copy-start = (bf16[128,1024]{1,0:T(8,128)(2,1)S(1)}, bf16[128,1024]{1,0:T(8,128)(2,1)}, u32[]{:S(2)}) copy-start(bf16[128,1024]{1,0:T(8,128)(2,1)} %q_hbm.1) | copy-start | bytes 786436
  2.3 0.9 %copy-start.1 = (bf16[128,1024]{1,0:T(8,128)(2,1)S(1)}, bf16[128,1024]{1,0:T(8,128)(2,1)}, u32[]{:S(2)}) copy-start(bf16[128,1024]{1,0:T(8,128)(2,1)} %k_hbm.1) | copy-start | bytes 786436
  3.2 0.9 %copy-start.2 = (bf16[128,1024]{1,0:T(8,128)(2,1)S(1)}, bf16[128,1024]{1,0:T(8,128)(2,1)}, u32[]{:S(2)}) copy-start(bf16[128,1024]{1,0:T(8,128)(2,1)} %v_hbm.1) | copy-start | bytes 786436
  4.2 0.9 %copy-start.3 = (bf16[128,1024]{1,0:T(8,128)(2,1)S(1)}, bf16[128,1024]{1,0:T(8,128)(2,1)}, u32[]{:S(2)}) copy-start(bf16[128,1024]{1,0:T(8,128)(2,1)} %dy_hbm.1) | copy-start | bytes 786436
  5.1 0.7 %copy-start.4 = (s32[2,8,8]{2,1,0:T(8,128)S(1)}, s32[2,8,8]{2,1,0:T(8,128)}, u32[]{:S(2)}) copy-start(s32[2,8,8]{2,1,0:T(8,128)} %table_ref.1) | copy-start | bytes 1540
  5.8 0.7 copy-start.5

commit v2 on v1

--- a/solution.py
+++ b/solution.py
@@ -28,9 +28,9 @@
 
 def kernel(
     ctx_count, head_count,
-    q_hbm, k_hbm, v_hbm, dy_hbm, kind_ref, table_ref, scale_ref, gain_ref,
+    q_hbm, k_hbm, v_hbm, dy_hbm, kind_hbm, table_hbm, scale_hbm, gain_hbm,
     att_ref, gq_ref, gk_ref, gv_ref,
-    q_ref, k_ref, v_ref, dy_ref, kind_col, inv_col, coef_col,
+    q_ref, k_ref, v_ref, dy_ref, kind_ref, table_ref, scale_ref, gain_ref, kind_col, inv_col, coef_col,
     states, probs, query_t, readout, grad_out_ref, kind_sums, grad_states, key_acc, value_acc,
     fwd_send, fwd_recv, bwd_send, bwd_recv, stat_send, stat_recv,
     load_sem, fwd_ssem, fwd_rsem, bwd_ssem, bwd_rsem, stat_ssem, stat_rsem,
@@ -54,7 +54,10 @@
     loads = [
         pltpu.make_async_copy(src, dst, load_sem.at[i])
         for i, (src, dst) in enumerate(
-            ((k_hbm, k_ref), (v_hbm, v_ref), (q_hbm, q_ref), (dy_hbm, dy_ref))
+            (
+                (k_hbm, k_ref), (v_hbm, v_ref), (q_hbm, q_ref), (dy_hbm, dy_ref),
+                (kind_hbm, kind_ref), (table_hbm, table_ref), (scale_hbm, scale_ref), (gain_hbm, gain_ref),
+            )
         )
     ]
     for load in loads:
@@ -113,8 +116,8 @@
         def _():
             fwd(0, j).start()
 
-    loads[2].wait()
-    loads[3].wait()
+    for load in loads[2:]:
+        load.wait()
     kind_col[...] = jnp.transpose(
         jnp.broadcast_to(kind_ref[...].astype(F32), (size, tokens))
     )
@@ -155,7 +158,7 @@
     for step in range(chunks + depth - 1):
         if step < chunks:
             local_forward(step)
-        for b in reversed(range(depth)):
+        for b in range(depth):
             j = step - b
             if 0 <= j < chunks:
                 receive_forward(b, j)
@@ -264,7 +267,7 @@
     for step in range(chunks + depth - 1):
         if step < chunks:
             local_backward(step)
-        for b in range(depth):
+        for b in reversed(range(depth)):
             j = step - (depth - 1 - b)
             if 0 <= j < chunks:
                 receive_backward(b, j)
@@ -293,17 +296,22 @@
         kinds, heads, _ = level_table.shape
         size = width // heads
         chunks = heads // CHUNK
-        anywhere = pl.BlockSpec(memory_space=pl.ANY)
+        hbm = pl.BlockSpec(memory_space=pltpu.HBM)
         vmem = pl.BlockSpec(memory_space=pltpu.VMEM)
-        smem = pl.BlockSpec(memory_space=pltpu.SMEM)
         block = jax.ShapeDtypeStruct((tokens, width), BF16)
         square = (heads, size, size)
         return pl.pallas_call(
             functools.partial(kernel, ctx_count, head_count),
             out_shape=(block,) * 4,
-            in_specs=[anywhere] * 4 + [vmem, smem, smem, vmem],
+            in_specs=[hbm] * 8,
             out_specs=(vmem,) * 4,
             scratch_shapes=[pltpu.VMEM((tokens, width), BF16)] * 4
+            + [
+                pltpu.VMEM((1, tokens), jnp.int32),
+                pltpu.SMEM(level_table.shape, jnp.int32),
+                pltpu.SMEM((heads,), F32),
+                pltpu.VMEM((1, width), F32),
+            ]
             + [pltpu.VMEM((tokens, size), F32)] * 3
             + [
                 pltpu.VMEM(square, F32),
@@ -320,12 +328,12 @@
             + [
                 pltpu.VMEM((8, tokens), F32),
                 pltpu.VMEM((head_count - 1, 8, tokens), F32),
-                pltpu.SemaphoreType.DMA((4,)),
+                pltpu.SemaphoreType.DMA((8,)),
             ]
             + [pltpu.SemaphoreType.DMA((depth, chunks))] * 4
             + [pltpu.SemaphoreType.DMA((head_count - 1,))] * 2,
             compiler_params=pltpu.CompilerParams(
-                collective_id=0, has_side_effects=True, vmem_limit_bytes=40 * 1024 * 1024
+                collective_id=0, has_side_effects=True, vmem_limit_bytes=64 * 1024 * 1024
             ),
             cost_estimate=pl.CostEstimate(
                 flops=36 * heads * tokens * size * size, bytes_accessed=16 * tokens * width, transcendentals=0

time: 69.7 us -> 54.5 us (0.78)
  Pallas kernels: 60.1 us -> 49.1 us
  local copies, waits for them, and re-layouts: 8.65 us -> 4.5 us
    pallas_call x1, Pallas kernels: 60.1 us -> 49.1 us  [shards(): pl.pallas_call(functools.partial(kernel, ctx_count, head_count), out_shap...]
    unnamed x20 -> x10, local copies, waits for them, and re-layouts: 8.65 us -> 4.5 us
where the time goes in v2:
time: 54.5 us; the launch traced here: 54.3 us
  Pallas kernels  49.1 us (90%)
  local copies, waits for them, and re-layouts  4.5 us (8%)
  between operations  0.65 us (1%)
    pallas_call x1, Pallas kernels, shards(): pl.pallas_call(functools.partial(kernel, ctx_count, head_count), out_shap...  49.1 us
    unnamed x10, local copies, waits for them, and re-layouts  4.5 us

profile of v2, /device:TPU:0, one launch (start us, length us, event | category | flops | bytes accessed | tf_op | source)
XLA Modules:
  0.0 54.3 jit_solution(4507389752164439107)
XLA Ops:
  0.6 49.1 %shard_map.111 = (bf16[128,1024]{1,0:T(8,128)(2,1)}, bf16[128,1024]{1,0:T(8,128)(2,1)}, bf16[128,1024]{1,0:T(8,128)(2,1)}, bf16[128,1024]{1,0:T(8,128)(2,1)}) custom-call(bf16[128,1024]{1,0:T(8,128)(2,1)} %q_hbm.1, bf16[128,1024]{1,0:T(8,128)(2,1)} %k_hbm.1, bf16[128,1024]{1,0:T(8,128)(2,1)} %v_hbm.1, bf16[128,1024]{1,0:T(8,128)(2,1)} %dy_hbm.1, ...), custom_call_target="tpu_custom_call" | custom-call | flops 603979776 | bytes 2097152 | tf_op jit(solution)/shard_map/pallas_call | solution.py:303
  49.8 0.0 copy-start.2
  49.8 1.7 %copy.16 = bf16[128,1024]{1,0:T(8,128)(2,1)} copy(bf16[128,1024]{1,0:T(8,128)(2,1)} %get-tuple-element.8) | data formatting | bytes 524288
  51.5 0.0 copy-done.2
  51.5 0.0 copy-start.1
  51.5 0.7 %copy.17 = bf16[128,1024]{1,0:T(8,128)(2,1)} copy(bf16[128,1024]{1,0:T(8,128)(2,1)S(1)} %copy-done.2) | data formatting | bytes 524288
  52.2 0.3 copy-done.1
  52.5 0.0 copy-start
  52.5 0.7 %copy.18 = bf16[128,1024]{1,0:T(8,128)(2,1)} copy(bf16[128,1024]{1,0:T(8,128)(2,1)S(1)} %copy-done.1) | data formatting | bytes 524288
  53.2 0.3 copy-done
  53.6 0.7 %copy.19 = bf16[128,1024]{1,0:T(8,128)(2,1)} copy(bf16[128,1024]{1,0:T(8,128)(2,1)S(1)} %copy-done) | data formatting | bytes 524288
Async XLA Ops:
  49.8 1.7 %copy-start.2 = (bf16[128,1024]{1,0:T(8,128)(2,1)S(1)}, bf16[128,1024]{1,0:T(8,128)(2,1)}, u32[]{:S(2)}) copy-start(bf16[128,1024]{1,0:T(8,128)(2,1)} %get-tuple-element.9) | copy-start | bytes 786436
  51.5 1.0 %copy-start.1 = (bf16[128,1024]{1,0:T(8,128)(2,1)S(1)}, bf16[128,1024]{1,0:T(8,128)(2,1)}, u32[]{:S(2)}) copy-start(bf16[128,1024]{1,0:T(8,128)(2,1)} %get-tuple-element.10) | copy-start | bytes 786436
  52.5 1.0 %copy-start = (bf16[128,1024]{1,0:T(8,128)(2,1)S(1)}, bf16[128,1024]{1,0:T(8,128)(2,1)}, u32[]{:S(2)}) copy-start(bf16[128,1024]{1,0:T(8,128)(2,1)} %get-tuple-element.11) | copy-start | bytes 786436

commit v3 on v2

v3 whole, which is shorter than its diff:
```python
import functools

import jax
import jax.numpy as jnp
from jax import lax
from jax.experimental import pallas as pl
from jax.experimental.pallas import tpu as pltpu
from jax.sharding import PartitionSpec as P

EPSILON = 1e-06
CHUNK = 2
F32 = jnp.float32
BF16 = jnp.bfloat16


def factor(level):
    return 0.25 * 2.0 ** (-0.5 * level)


def dot(left, right, contract):
    return lax.dot_general(left, right, (contract, ((), ())), preferred_element_type=F32)


NN = ((1,), (0,))
NT = ((1,), (1,))
TN = ((0,), (0,))


def kernel(
    ctx_count, head_count,
    q_hbm, k_hbm, v_hbm, dy_hbm, kind_hbm, table_hbm, scale_hbm, gain_hbm,
    att_hbm, gq_hbm, gk_hbm, gv_hbm,
    q_ref, k_ref, v_ref, dy_ref, kind_ref, table_ref, scale_ref, gain_ref,
    att_ref, gq_ref, gk_ref, gv_ref, kind_col, inv_col, coef_col,
    states, probs, query_t, readout, grad_out_ref, kind_sums, grad_states, key_acc, value_acc,
    own_send, total_send, fwd_recv, half_send, half_recv, back_send, back_recv, last_send, last_recv,
    stat_send, stat_recv,
    load_sem, store_sem, own_ssem, total_ssem, relay_ssem, fwd_rsem, half_ssem, half_rsem,
    back_ssem, back_rsem, last_ssem, last_rsem, stat_ssem, stat_rsem,
):
    tokens, width = q_ref.shape
    heads, size, _ = states.shape
    kinds = table_ref.shape[0]
    depth = ctx_count.bit_length() - 1
    pairs = ctx_count // 2
    half = heads // 2
    parts = half // CHUNK
    c = lax.axis_index("ctx")
    me = lax.axis_index("head")
    pair, side = c >> 1, c & 1
    mesh_id = pl.DeviceIdType.MESH
    odd = side == 1
    inner = pair != pairs - 1
    upper = [((c >> b) & 1) == 1 for b in range(depth)]
    source = [None] + [(pair & ((1 << b) - 1)) == (1 << (b - 1)) - 1 for b in range(1, depth)]
    above = [None] + [
        jnp.logical_and(inner, (pair & ((1 << b) - 1)) == (1 << b) - 1) for b in range(1, depth)
    ]
    place = [None] + [pair & ((1 << (b - 1)) - 1) for b in range(1, depth)]
    origin = [None] + [pair - place[b] - 1 for b in range(1, depth)]
    beside = {"ctx": c ^ 1}

    def at_pair(other):
        return {"ctx": 2 * other + side}

    loads = [
        pltpu.make_async_copy(src, dst, load_sem.at[i])
        for i, (src, dst) in enumerate(
            (
                (k_hbm, k_ref), (v_hbm, v_ref), (q_hbm, q_ref), (dy_hbm, dy_ref),
                (kind_hbm, kind_ref), (table_hbm, table_ref), (scale_hbm, scale_ref), (gain_hbm, gain_ref),
            )
        )
    ]
    for load in loads:
        load.start()

    barrier = pltpu.get_barrier_semaphore()

    def greet(device):
        pl.semaphore_signal(barrier, inc=1, device_id=device, device_id_type=mesh_id)

    greet(beside)
    for d in range(1, head_count):
        greet({"head": lax.rem(me + d, head_count)})
    greeted = head_count
    for b in range(1, depth):

        @pl.when(upper[b])
        def _():
            greet(at_pair(origin[b]))

        @pl.when(source[b])
        def _():
            for t in range(1 << (b - 1)):
                greet(at_pair(pair + 1 + t))

        greeted = greeted + ((c >> b) & 1) + jnp.where(source[b], 1 << (b - 1), 0)

    def first_chunk(mine, jj):
        return (side if mine else 1 - side) * parts + jj

    def chunk_heads(mine, jj):
        first = first_chunk(mine, jj) * CHUNK
        return [first + i for i in range(CHUNK)]

    def part(mine, jj):
        return pl.ds(first_chunk(mine, jj) * CHUNK, CHUNK)

    def cols(h):
        return pl.ds(pl.multiple_of(h * size, size), size)

    def remote(src, dst, ssem, rsem, device):
        return pltpu.make_async_remote_copy(
            src_ref=src, dst_ref=dst, send_sem=ssem, recv_sem=rsem, device_id=device, device_id_type=mesh_id
        )

    def own_copy(mine, jj):
        at, j = part(mine, jj), first_chunk(mine, jj)
        return remote(own_send.at[at], fwd_recv.at[0, at], own_ssem.at[j], fwd_rsem.at[0, j], beside)

    def total_copy(b, t, mine, jj):
        at, j = part(mine, jj), first_chunk(mine, jj)
        return remote(
            total_send.at[at], fwd_recv.at[b, at], total_ssem.at[t, j], fwd_rsem.at[b, j], at_pair(pair + 1 + t)
        )

    def relay_copy(b, mine, jj):
        at, j = part(mine, jj), first_chunk(mine, jj)
        return remote(fwd_recv.at[b, at], fwd_recv.at[b, at], relay_ssem.at[b, j], fwd_rsem.at[b, j], beside)

    def half_copy(b, mine, jj):
        at, j = part(mine, jj), first_chunk(mine, jj)
        return remote(half_send.at[b, at], half_recv.at[b, at], half_ssem.at[b, j], half_rsem.at[b, j], beside)

    def back_copy(b, mine, jj):
        at, j = part(mine, jj), first_chunk(mine, jj)
        return remote(
            back_send.at[b, at], back_recv.at[place[b], at], back_ssem.at[b, j], back_rsem.at[place[b], j],
            at_pair(origin[b]),
        )

    def back_arrival(t, mine, jj):
        at, j = part(mine, jj), first_chunk(mine, jj)
        return remote(back_send.at[0, at], back_recv.at[t, at], back_ssem.at[0, j], back_rsem.at[t, j], beside)

    def last_copy(mine, jj):
        at, j = part(mine, jj), first_chunk(mine, jj)
        return remote(last_send.at[at], last_recv.at[at], last_ssem.at[j], last_rsem.at[j], beside)

    def takes(mine):
        return jnp.logical_or(odd, jnp.logical_and(inner, True if mine else source[1]))

    def gives(mine):
        return jnp.logical_or(side == 0, jnp.logical_and(inner, source[1] if mine else True))

    chunk_list = [(mine, jj) for mine in (False, True) for jj in range(parts)]

    def weight(kind, h, level):
        return table_ref[kind, h, level].astype(F32) * factor(level)

    def token_weights(h, level):
        out = jnp.full((tokens, size), weight(0, h, level), F32)
        for kind in range(1, kinds):
            out = jnp.where(kind_col[...] == kind, weight(kind, h, level), out)
        return out

    def causal():
        row = lax.broadcasted_iota(jnp.int32, (tokens, tokens), 0)
        col = lax.broadcasted_iota(jnp.int32, (tokens, tokens), 1)
        return col <= row

    loads[0].wait()
    loads[1].wait()
    for index, (mine, jj) in enumerate(chunk_list):
        for h in chunk_heads(mine, jj):
            state = dot(k_ref[:, cols(h)], v_ref[:, cols(h)], TN)
            states[h] = state
            own_send[h] = state.astype(BF16)
        if index == 0:
            pl.semaphore_wait(barrier, greeted)

        @pl.when(gives(mine))
        def _():
            own_copy(mine, jj).start()

    for load in loads[2:]:
        load.wait()
    kind_col[...] = jnp.transpose(
        jnp.broadcast_to(kind_ref[...].astype(F32), (size, tokens))
    )

    def local_forward(mine, jj):
        for h in chunk_heads(mine, jj):
            q = q_ref[:, cols(h)]
            scores = dot(q, k_ref[:, cols(h)], NT)
            attn = (jnp.where(causal(), scores, 0.0) * token_weights(h, 0)).astype(BF16)
            probs[h] = attn
            readout[h] = dot(attn, v_ref[:, cols(h)], NN)
            query_t[h] = jnp.transpose(q)

    def send_total(b, mine, jj):
        for h in chunk_heads(mine, jj):
            total_send[h] = states[h].astype(BF16)
        for t in reversed(range(1 << (b - 1))):
            total_copy(b, t, mine, jj).start()

    def add_level(b, mine, jj):
        for h in chunk_heads(mine, jj):
            level = dot(q_ref[:, cols(h)], fwd_recv[b, h], NN)
            readout[h] += token_weights(h, b + 1) * level

    def add_state(b, mine, jj):
        for h in chunk_heads(mine, jj):
            states[h] += fwd_recv[b, h].astype(F32)

    def receive_first(mine, jj):
        @pl.when(takes(mine))
        def _():
            own_copy(mine, jj).wait_recv()
            add_state(0, mine, jj)

        if depth > 1:

            @pl.when(source[1])
            def _():
                send_total(1, mine, jj)

        @pl.when(odd)
        def _():
            add_level(0, mine, jj)

    def receive_total(b, mine, jj):
        @pl.when(upper[b])
        def _():
            total_copy(b, 0, mine, jj).wait_recv()
            if b > 1 and mine:
                relay_copy(b, mine, jj).start()

        if mine and b + 1 < depth:

            @pl.when(above[b])
            def _():
                add_state(b, mine, jj)

            @pl.when(source[b + 1])
            def _():
                send_total(b + 1, mine, jj)

        @pl.when(upper[b])
        def _():
            add_level(b, mine, jj)

    events = []
    stride = 3 * parts + 5
    for jj in range(parts):
        events += [
            (0.5 + jj, local_forward, (True, jj)),
            (0.5 + jj + parts, local_forward, (False, jj)),
            (1.0 + jj, receive_first, (True, jj)),
            (1.0 + jj + parts, receive_first, (False, jj)),
        ]
        if depth > 1:
            events += [
                (2.3 + jj, receive_total, (1, True, jj)),
                (2.3 + jj + parts, receive_total, (1, False, jj)),
            ]
        for b in range(2, depth):
            now = 4.6 + 2 * jj + (b - 2) * stride
            events += [
                (now, receive_total, (b, True, jj)),
                (now + 1.4, receive_total, (b, False, jj)),
            ]
    for _, event, at in sorted(events, key=lambda item: item[0]):
        event(*at)

    squares = jnp.zeros((tokens, size), F32)
    crosses = jnp.zeros((tokens, size), F32)
    for mine, jj in chunk_list:
        for h in chunk_heads(mine, jj):
            z = readout[h] * scale_ref[h]
            readout[h] = z
            squares += z * z
            crosses += gain_ref[:, cols(h)] * dy_ref[:, cols(h)].astype(F32) * z

    stat_send[0:1, :] = jnp.sum(jnp.transpose(squares), axis=0, keepdims=True)
    stat_send[1:2, :] = jnp.sum(jnp.transpose(crosses), axis=0, keepdims=True)
    stat_copies = [
        remote(
            stat_send, stat_recv.at[d - 1], stat_ssem.at[d - 1], stat_rsem.at[d - 1],
            {"head": lax.rem(me + d, head_count)},
        )
        for d in range(1, head_count)
    ]
    for copy in stat_copies:
        copy.start()
    square_row = stat_send[0:1, :]
    cross_row = stat_send[1:2, :]
    for d, copy in enumerate(stat_copies):
        copy.wait_recv()
        square_row += stat_recv[d, 0:1, :]
        cross_row += stat_recv[d, 1:2, :]
    features = width * head_count
    rms = jnp.sqrt(square_row / features + EPSILON)
    coef = cross_row / (features * rms * rms * rms)
    inv_col[...] = jnp.transpose(jnp.broadcast_to(1.0 / rms, (size, tokens)))
    coef_col[...] = jnp.transpose(jnp.broadcast_to(coef, (size, tokens)))

    def message(b, h, flag=1.0):
        total = None
        for kind in range(kinds):
            term = (weight(kind, h, b + 1) * flag) * kind_sums[h, :, pl.ds(kind * size, size)]
            total = term if total is None else total + term
        return total

    def send_bucket_grad(mine, jj):
        for h in chunk_heads(mine, jj):
            back_send[1, h] = (grad_states[h] + message(1, h)).astype(BF16)
        back_copy(1, mine, jj).start()

    for mine, jj in chunk_list:
        for h in chunk_heads(mine, jj):
            gain = gain_ref[:, cols(h)]
            z = readout[h]
            att_ref[:, cols(h)] = (z * inv_col[...] * gain).astype(BF16)
            grad = gain * dy_ref[:, cols(h)].astype(F32) * inv_col[...] - z * coef_col[...]
            grad = (grad * scale_ref[h]).astype(BF16)
            grad_out_ref[h] = grad
            masked = jnp.concatenate(
                [jnp.where(kind_col[...] == kind, grad.astype(F32), 0.0).astype(BF16) for kind in range(kinds)],
                axis=1,
            )
            kind_sums[h] = dot(query_t[h], masked, NN)
            grad_states[h] = jnp.zeros((size, size), F32)
        if not mine:
            for b in reversed(range(2, depth)):

                @pl.when(upper[b])
                def _():
                    for h in chunk_heads(mine, jj):
                        half_send[b, h] = message(b, h).astype(BF16)
                    half_copy(b, mine, jj).start()

        if depth > 1:

            @pl.when(jnp.logical_and(upper[1], jnp.logical_not(above[1])) if mine else upper[1])
            def _():
                send_bucket_grad(mine, jj)

    stores = [
        pltpu.make_async_copy(src, dst, store_sem.at[i])
        for i, (src, dst) in enumerate(
            ((att_ref, att_hbm), (gq_ref, gq_hbm), (gk_ref, gk_hbm), (gv_ref, gv_hbm))
        )
    ]
    stores[0].start()

    def local_backward(mine, jj):
        for h in chunk_heads(mine, jj):
            grad = grad_out_ref[h]
            scores = dot(grad, v_ref[:, cols(h)], NT)
            dprobs = (jnp.where(causal(), scores, 0.0) * token_weights(h, 0)).astype(BF16)
            key_acc[h] = dot(dprobs, q_ref[:, cols(h)], TN)
            value_acc[h] = dot(probs[h], grad, TN)
            readout[h] = dot(dprobs, k_ref[:, cols(h)], NN)
        for b in range(depth):

            @pl.when(upper[b])
            def _():
                for h in chunk_heads(mine, jj):
                    level = dot(grad_out_ref[h], fwd_recv[b, h], NT)
                    readout[h] += token_weights(h, b + 1) * level

        for h in chunk_heads(mine, jj):
            gq_ref[:, cols(h)] = readout[h].astype(BF16)

    def pass_half(b, jj):
        @pl.when(upper[b])
        def _():
            half_copy(b, True, jj).wait_recv()
            for h in chunk_heads(True, jj):
                total = grad_states[h] + message(b, h) + half_recv[b, h].astype(F32)
                back_send[b, h] = total.astype(BF16)
            back_copy(b, True, jj).start()

    def gather_grads(b, mine, jj):
        @pl.when(source[b])
        def _():
            for t in range(1 << (b - 1)):
                back_arrival(t, mine, jj).wait_recv()
                for h in chunk_heads(mine, jj):
                    grad_states[h] += back_recv[t, h].astype(F32)

    def pass_bucket_grad(jj):
        @pl.when(jnp.logical_and(upper[1], above[1]))
        def _():
            send_bucket_grad(True, jj)

    def send_last(mine, jj):
        @pl.when(takes(mine))
        def _():
            flag = side.astype(F32)
            for h in chunk_heads(mine, jj):
                last_send[h] = (grad_states[h] + message(0, h, flag)).astype(BF16)
            last_copy(mine, jj).start()

    def finish(mine, jj):
        @pl.when(gives(mine))
        def _():
            last_copy(mine, jj).wait_recv()
            for h in chunk_heads(mine, jj):
                grad_states[h] += last_recv[h].astype(F32)

        for h in chunk_heads(mine, jj):
            state = grad_states[h].astype(BF16)
            gk_ref[:, cols(h)] = (key_acc[h] + dot(v_ref[:, cols(h)], state, NT)).astype(BF16)
            gv_ref[:, cols(h)] = (value_acc[h] + dot(k_ref[:, cols(h)], state, NN)).astype(BF16)

    events = []
    late = max(depth - 3, 0) * stride
    for jj in range(parts):
        for b in range(2, depth):
            now = (depth - 1 - b) * stride
            events += [
                (now + 1.0 + jj, pass_half, (b, jj)),
                (now + 3.3 + 2 * jj, gather_grads, (b, True, jj)),
            ]
        if depth > 1:
            events += [
                (late + 3.4 + 2 * jj, pass_bucket_grad, (jj,)),
                (late + 2.5 + jj, gather_grads, (1, False, jj)),
                (late + 4.7 + 2 * jj, gather_grads, (1, True, jj)),
            ]
        events += [
            (0.9 + 0.2 * jj, local_backward, (False, jj)),
            (2.3 + 0.2 * jj, local_backward, (True, jj)),
            (late + 2.6 + jj, send_last, (False, jj)),
            (late + 4.8 + 2 * jj, send_last, (True, jj)),
            (late + 5.0 + 2 * jj, finish, (True, jj)),
            (late + 5.9 + 2 * jj, finish, (False, jj)),
        ]
    for _, event, at in sorted(events, key=lambda item: item[0]):
        event(*at)
    for store in stores[1:]:
        store.start()

    for copy in stat_copies:
        copy.wait_send()
    for mine, jj in chunk_list:

        @pl.when(gives(mine))
        def _():
            own_copy(mine, jj).wait_send()

        @pl.when(takes(mine))
        def _():
            last_copy(mine, jj).wait_send()

        for b in range(1, depth):
            if mine or b == 1:

                @pl.when(source[b])
                def _():
                    for t in range(1 << (b - 1)):
                        total_copy(b, t, mine, jj).wait_send()

                @pl.when(upper[b])
                def _():
                    back_copy(b, mine, jj).wait_send()
                    if b > 1:
                        relay_copy(b, mine, jj).wait_send()

            else:

                @pl.when(upper[b])
                def _():
                    half_copy(b, mine, jj).wait_send()

    for store in stores:
        store.wait()


def land(*refs):
    count = (len(refs) - 1) // 2
    copies = [
        pltpu.make_async_copy(refs[i], refs[count + i], refs[-1].at[i]) for i in range(count)
    ]
    for copy in copies:
        copy.start()
    for copy in copies:
        copy.wait()


def solution(mesh):
    ctx_count, head_count = mesh.shape["ctx"], mesh.shape["head"]
    depth = ctx_count.bit_length() - 1
    targets = max(ctx_count // 4, 1)

    def shards(queries, keys, values, grad_out, token_kind, level_table, head_scale, norm_gain):
        tokens, width = queries.shape
        kinds, heads, _ = level_table.shape
        size = width // heads
        chunks = heads // CHUNK
        hbm = pl.BlockSpec(memory_space=pltpu.HBM)
        block = jax.ShapeDtypeStruct((tokens, width), BF16)
        square = (heads, size, size)
        dma = pltpu.SemaphoreType.DMA
        results = pl.pallas_call(
            functools.partial(kernel, ctx_count, head_count),
            out_shape=(block,) * 4,
            in_specs=[hbm] * 8,
            out_specs=(hbm,) * 4,
            scratch_shapes=[pltpu.VMEM((tokens, width), BF16)] * 4
            + [
                pltpu.VMEM((1, tokens), jnp.int32),
                pltpu.SMEM(level_table.shape, jnp.int32),
                pltpu.SMEM((heads,), F32),
                pltpu.VMEM((1, width), F32),
            ]
            + [pltpu.VMEM((tokens, width), BF16)] * 4
            + [pltpu.VMEM((tokens, size), F32)] * 3
            + [
                pltpu.VMEM(square, F32),
                pltpu.VMEM((heads, tokens, tokens), BF16),
                pltpu.VMEM((heads, size, tokens), BF16),
                pltpu.VMEM((heads, tokens, size), F32),
                pltpu.VMEM((heads, tokens, size), BF16),
                pltpu.VMEM((heads, size, kinds * size), F32),
                pltpu.VMEM(square, F32),
                pltpu.VMEM((heads, tokens, size), F32),
                pltpu.VMEM((heads, tokens, size), F32),
                pltpu.VMEM(square, BF16),
                pltpu.VMEM(square, BF16),
                pltpu.VMEM((depth,) + square, BF16),
                pltpu.VMEM((depth,) + square, BF16),
                pltpu.VMEM((depth,) + square, BF16),
                pltpu.VMEM((depth,) + square, BF16),
                pltpu.VMEM((targets,) + square, BF16),
                pltpu.VMEM(square, BF16),
                pltpu.VMEM(square, BF16),
                pltpu.VMEM((8, tokens), F32),
                pltpu.VMEM((head_count - 1, 8, tokens), F32),
                dma((8,)),
                dma((4,)),
                dma((chunks,)),
                dma((targets, chunks)),
                dma((depth, chunks)),
                dma((depth, chunks)),
                dma((depth, chunks)),
                dma((depth, chunks)),
                dma((depth, chunks)),
                dma((targets, chunks)),
                dma((chunks,)),
                dma((chunks,)),
                dma((head_count - 1,)),
                dma((head_count - 1,)),
            ],
            compiler_params=pltpu.CompilerParams(
                collective_id=0, has_side_effects=True, vmem_limit_bytes=64 * 1024 * 1024
            ),
            cost_estimate=pl.CostEstimate(
                flops=36 * heads * tokens * size * size, bytes_accessed=16 * tokens * width, transcendentals=0
            ),
        )(
            queries, keys, values, grad_out,
            token_kind.reshape(1, tokens), level_table, head_scale, norm_gain.reshape(1, width),
        )
        return pl.pallas_call(
            land,
            out_shape=(block,) * 4,
            in_specs=[hbm] * 4,
            out_specs=(hbm,) * 4,
            scratch_shapes=[dma((4,))],
            compiler_params=pltpu.CompilerParams(vmem_limit_bytes=64 * 1024 * 1024),
        )(*results)

    in_specs = (
        P("ctx", "head"),
        P("ctx", "head"),
        P("ctx", "head"),
        P("ctx", "head"),
        P("ctx"),
        P(None, "head", None),
        P("head"),
        P("head"),
    )
    return jax.shard_map(
        shards, mesh=mesh, in_specs=in_specs, out_specs=(P("ctx", "head"),) * 4, check_vma=False
    )
```

time: 54.5 us -> 84.2 us (1.54)
  Pallas kernels: 49.1 us -> 83.5 us
  local copies, waits for them, and re-layouts: 4.5 us -> 0 us
    pallas_call x0 -> x1, Pallas kernels: none -> 32.9 us  [shards(): pl.pallas_call(land, out_shape=(block,) * 4, in_specs=[hbm] * 4, out_spec...]
    unnamed x10 -> x0, local copies, waits for them, and re-layouts: 4.5 us -> none
    pallas_call x1, Pallas kernels: 49.1 us -> 50.5 us  [shards(): pl.pallas_call(functools.partial(kernel, ctx_count, head_count), out_shap...]
where the time goes in v3:
time: 84.2 us; the launch traced here: 84.1 us
  Pallas kernels  83.5 us (99%)
    pallas_call x1, Pallas kernels, shards(): pl.pallas_call(functools.partial(kernel, ctx_count, head_count), out_shap...  50.5 us
    pallas_call x1, Pallas kernels, shards(): pl.pallas_call(land, out_shape=(block,) * 4, in_specs=[hbm] * 4, out_spec...  32.9 us

profile of v3, /device:TPU:0, one launch (start us, length us, event | category | flops | bytes accessed | tf_op | source)
XLA Modules:
  0.0 84.1 jit_solution(8757412219301843971)
XLA Ops:
  0.6 50.5 %shard_map.111 = (bf16[128,1024]{1,0:T(8,128)(2,1)}, bf16[128,1024]{1,0:T(8,128)(2,1)}, bf16[128,1024]{1,0:T(8,128)(2,1)}, bf16[128,1024]{1,0:T(8,128)(2,1)}) custom-call(bf16[128,1024]{1,0:T(8,128)(2,1)} %q_hbm.1, bf16[128,1024]{1,0:T(8,128)(2,1)} %k_hbm.1, bf16[128,1024]{1,0:T(8,128)(2,1)} %v_hbm.1, bf16[128,1024]{1,0:T(8,128)(2,1)} %dy_hbm.1, ...), custom_call_target="tpu_custom_call" | custom-call | flops 603979776 | bytes 2097152 | tf_op jit(solution)/shard_map/pallas_call | solution.py:508
  51.2 32.9 %shard_map.112 = (bf16[128,1024]{1,0:T(8,128)(2,1)}, bf16[128,1024]{1,0:T(8,128)(2,1)}, bf16[128,1024]{1,0:T(8,128)(2,1)}, bf16[128,1024]{1,0:T(8,128)(2,1)}) custom-call(bf16[128,1024]{1,0:T(8,128)(2,1)} %get-tuple-element.8.refs_0_, bf16[128,1024]{1,0:T(8,128)(2,1)} %get-tuple-element.9.refs_1_, bf16[128,1024]{1,0:T(8,128)(2,1)} %get-tuple-element.10.refs_2_, ...), custom_call_target="tpu_custom_call" | custom-call | tf_op jit(solution)/shard_map/pallas_call | solution.py:568

commit v4 on v3

--- a/solution.py
+++ b/solution.py
@@ -8,7 +8,8 @@
 from jax.sharding import PartitionSpec as P
 
 EPSILON = 1e-06
-CHUNK = 2
+CHUNK = 1
+GROUP = 2
 F32 = jnp.float32
 BF16 = jnp.bfloat16
 
@@ -100,9 +101,8 @@
     def first_chunk(mine, jj):
         return (side if mine else 1 - side) * parts + jj
 
-    def chunk_heads(mine, jj):
-        first = first_chunk(mine, jj) * CHUNK
-        return [first + i for i in range(CHUNK)]
+    def chunk_heads(mine, *several):
+        return [first_chunk(mine, jj) * CHUNK + i for jj in several for i in range(CHUNK)]
 
     def part(mine, jj):
         return pl.ds(first_chunk(mine, jj) * CHUNK, CHUNK)
@@ -155,6 +155,7 @@
         return jnp.logical_or(side == 0, jnp.logical_and(inner, source[1] if mine else True))
 
     chunk_list = [(mine, jj) for mine in (False, True) for jj in range(parts)]
+    groups = [tuple(range(jj, min(jj + GROUP, parts))) for jj in range(0, parts, GROUP)]
 
     def weight(kind, h, level):
         return table_ref[kind, h, level].astype(F32) * factor(level)
@@ -190,8 +191,8 @@
         jnp.broadcast_to(kind_ref[...].astype(F32), (size, tokens))
     )
 
-    def local_forward(mine, jj):
-        for h in chunk_heads(mine, jj):
+    def local_forward(mine, group):
+        for h in chunk_heads(mine, *group):
             q = q_ref[:, cols(h)]
             scores = dot(q, k_ref[:, cols(h)], NT)
             attn = (jnp.where(causal(), scores, 0.0) * token_weights(h, 0)).astype(BF16)
@@ -205,10 +206,12 @@
         for t in reversed(range(1 << (b - 1))):
             total_copy(b, t, mine, jj).start()
 
-    def add_level(b, mine, jj):
-        for h in chunk_heads(mine, jj):
-            level = dot(q_ref[:, cols(h)], fwd_recv[b, h], NN)
-            readout[h] += token_weights(h, b + 1) * level
+    def add_level(b, mine, group):
+        @pl.when(upper[b])
+        def _():
+            for h in chunk_heads(mine, *group):
+                level = dot(q_ref[:, cols(h)], fwd_recv[b, h], NN)
+                readout[h] += token_weights(h, b + 1) * level
 
     def add_state(b, mine, jj):
         for h in chunk_heads(mine, jj):
@@ -226,10 +229,6 @@
             def _():
                 send_total(1, mine, jj)
 
-        @pl.when(odd)
-        def _():
-            add_level(0, mine, jj)
-
     def receive_total(b, mine, jj):
         @pl.when(upper[b])
         def _():
@@ -247,30 +246,27 @@
             def _():
                 send_total(b + 1, mine, jj)
 
-        @pl.when(upper[b])
-        def _():
-            add_level(b, mine, jj)
-
     events = []
     stride = 3 * parts + 5
-    for jj in range(parts):
-        events += [
-            (0.5 + jj, local_forward, (True, jj)),
-            (0.5 + jj + parts, local_forward, (False, jj)),
-            (1.0 + jj, receive_first, (True, jj)),
-            (1.0 + jj + parts, receive_first, (False, jj)),
-        ]
-        if depth > 1:
+    for mine in (True, False):
+        skip = 0 if mine else parts
+        for group in groups:
             events += [
-                (2.3 + jj, receive_total, (1, True, jj)),
-                (2.3 + jj + parts, receive_total, (1, False, jj)),
+                (0.5 + group[0] + skip, local_forward, (mine, group)),
+                (1.4 + group[-1] + skip, add_level, (0, mine, group)),
             ]
-        for b in range(2, depth):
-            now = 4.6 + 2 * jj + (b - 2) * stride
-            events += [
-                (now, receive_total, (b, True, jj)),
-                (now + 1.4, receive_total, (b, False, jj)),
-            ]
+            if depth > 1:
+                events += [(2.7 + group[-1] + skip, add_level, (1, mine, group))]
+            for b in range(2, depth):
+                now = 4.6 + 2 * group[-1] + (b - 2) * stride + (0 if mine else 1.4)
+                events += [(now + 0.1, add_level, (b, mine, group))]
+        for jj in range(parts):
+            events += [(1.0 + jj + skip, receive_first, (mine, jj))]
+            if depth > 1:
+                events += [(2.3 + jj + skip, receive_total, (1, mine, jj))]
+            for b in range(2, depth):
+                now = 4.6 + 2 * jj + (b - 2) * stride + (0 if mine else 1.4)
+                events += [(now, receive_total, (b, mine, jj))]
     for _, event, at in sorted(events, key=lambda item: item[0]):
         event(*at)
 
@@ -318,8 +314,8 @@
             back_send[1, h] = (grad_states[h] + message(1, h)).astype(BF16)
         back_copy(1, mine, jj).start()
 
-    for mine, jj in chunk_list:
-        for h in chunk_heads(mine, jj):
+    for mine, group in [(mine, group) for mine in (False, True) for group in groups]:
+        for h in chunk_heads(mine, *group):
             gain = gain_ref[:, cols(h)]
             z = readout[h]
             att_ref[:, cols(h)] = (z * inv_col[...] * gain).astype(BF16)
@@ -337,15 +333,17 @@
 
                 @pl.when(upper[b])
                 def _():
-                    for h in chunk_heads(mine, jj):
-                        half_send[b, h] = message(b, h).astype(BF16)
-                    half_copy(b, mine, jj).start()
+                    for jj in group:
+                        for h in chunk_heads(mine, jj):
+                            half_send[b, h] = message(b, h).astype(BF16)
+                        half_copy(b, mine, jj).start()
 
         if depth > 1:
 
             @pl.when(jnp.logical_and(upper[1], jnp.logical_not(above[1])) if mine else upper[1])
             def _():
-                send_bucket_grad(mine, jj)
+                for jj in group:
+                    send_bucket_grad(mine, jj)
 
     stores = [
         pltpu.make_async_copy(src, dst, store_sem.at[i])
@@ -355,8 +353,8 @@
     ]
     stores[0].start()
 
-    def local_backward(mine, jj):
-        for h in chunk_heads(mine, jj):
+    def local_backward(mine, group):
+        for h in chunk_heads(mine, *group):
             grad = grad_out_ref[h]
             scores = dot(grad, v_ref[:, cols(h)], NT)
             dprobs = (jnp.where(causal(), scores, 0.0) * token_weights(h, 0)).astype(BF16)
@@ -367,11 +365,11 @@
 
             @pl.when(upper[b])
             def _():
-                for h in chunk_heads(mine, jj):
+                for h in chunk_heads(mine, *group):
                     level = dot(grad_out_ref[h], fwd_recv[b, h], NT)
                     readout[h] += token_weights(h, b + 1) * level
 
-        for h in chunk_heads(mine, jj):
+        for h in chunk_heads(mine, *group):
             gq_ref[:, cols(h)] = readout[h].astype(BF16)
 
     def pass_half(b, jj):
@@ -418,6 +416,11 @@
 
     events = []
     late = max(depth - 3, 0) * stride
+    for group in groups:
+        events += [
+            (0.9 + group[0], local_backward, (False, group)),
+            (4.9 + 0.5 * group[0], local_backward, (True, group)),
+        ]
     for jj in range(parts):
         for b in range(2, depth):
             now = (depth - 1 - b) * stride
@@ -432,8 +435,6 @@
                 (late + 4.7 + 2 * jj, gather_grads, (1, True, jj)),
             ]
         events += [
-            (0.9 + 0.2 * jj, local_backward, (False, jj)),
-            (2.3 + 0.2 * jj, local_backward, (True, jj)),
             (late + 2.6 + jj, send_last, (False, jj)),
             (late + 4.8 + 2 * jj, send_last, (True, jj)),
             (late + 5.0 + 2 * jj, finish, (True, jj)),
@@ -481,14 +482,9 @@
 
 
 def land(*refs):
-    count = (len(refs) - 1) // 2
-    copies = [
-        pltpu.make_async_copy(refs[i], refs[count + i], refs[-1].at[i]) for i in range(count)
-    ]
-    for copy in copies:
-        copy.start()
-    for copy in copies:
-        copy.wait()
+    count = len(refs) // 2
+    for source, target in zip(refs[:count], refs[count:]):
+        target[...] = source[...]
 
 
 def solution(mesh):
@@ -565,12 +561,13 @@
             queries, keys, values, grad_out,
             token_kind.reshape(1, tokens), level_table, head_scale, norm_gain.reshape(1, width),
         )
+        rows = pl.BlockSpec((tokens // 2, width), lambda i: (i, 0))
         return pl.pallas_call(
             land,
             out_shape=(block,) * 4,
-            in_specs=[hbm] * 4,
-            out_specs=(hbm,) * 4,
-            scratch_shapes=[dma((4,))],
+            grid=(2,),
+            in_specs=[rows] * 4,
+            out_specs=(rows,) * 4,
             compiler_params=pltpu.CompilerParams(vmem_limit_bytes=64 * 1024 * 1024),
         )(*results)
 

time: 84.2 us -> 60.1 us (0.71)
  Pallas kernels: 83.5 us -> 59.2 us
    pallas_call x1, Pallas kernels: 32.9 us -> 2.13 us  [shards(): pl.pallas_call(land, out_shape=(block,) * 4, grid=(2,), in_specs=[rows] *...]
    pallas_call x1, Pallas kernels: 50.5 us -> 57.1 us  [shards(): pl.pallas_call(functools.partial(kernel, ctx_count, head_count), out_shap...]
where the time goes in v4:
time: 60.1 us; the launch traced here: 59.9 us
  Pallas kernels  59.2 us (99%)
  between operations  0.64 us (1%)
    pallas_call x1, Pallas kernels, shards(): pl.pallas_call(functools.partial(kernel, ctx_count, head_count), out_shap...  57.1 us
    pallas_call x1, Pallas kernels, shards(): pl.pallas_call(land, out_shape=(block,) * 4, grid=(2,), in_specs=[rows] *...  2.13 us

profile of v4, /device:TPU:0, one launch (start us, length us, event | category | flops | bytes accessed | tf_op | source)
XLA Modules:
  0.0 59.9 jit_solution(11974793324349725772)
XLA Ops:
  0.6 57.1 %shard_map.111 = (bf16[128,1024]{1,0:T(8,128)(2,1)}, bf16[128,1024]{1,0:T(8,128)(2,1)}, bf16[128,1024]{1,0:T(8,128)(2,1)}, bf16[128,1024]{1,0:T(8,128)(2,1)}) custom-call(bf16[128,1024]{1,0:T(8,128)(2,1)} %q_hbm.1, bf16[128,1024]{1,0:T(8,128)(2,1)} %k_hbm.1, bf16[128,1024]{1,0:T(8,128)(2,1)} %v_hbm.1, bf16[128,1024]{1,0:T(8,128)(2,1)} %dy_hbm.1, ...), custom_call_target="tpu_custom_call" | custom-call | flops 603979776 | bytes 2097152 | tf_op jit(solution)/shard_map/pallas_call | solution.py:504
  57.8 2.1 %shard_map.112 = (bf16[128,1024]{1,0:T(8,128)(2,1)}, bf16[128,1024]{1,0:T(8,128)(2,1)}, bf16[128,1024]{1,0:T(8,128)(2,1)}, bf16[128,1024]{1,0:T(8,128)(2,1)}) custom-call(bf16[128,1024]{1,0:T(8,128)(2,1)} %get-tuple-element.8.refs_0_, bf16[128,1024]{1,0:T(8,128)(2,1)} %get-tuple-element.9.refs_1_, bf16[128,1024]{1,0:T(8,128)(2,1)} %get-tuple-element.10.refs_2_, ...), custom_call_target="tpu_custom_call" | custom-call | tf_op jit(solution)/shard_map/pallas_call | solution.py:565

commit v5 on v4

--- a/solution.py
+++ b/solution.py
@@ -8,8 +8,8 @@
 from jax.sharding import PartitionSpec as P
 
 EPSILON = 1e-06
-CHUNK = 1
-GROUP = 2
+CHUNK = 4
+GROUP = 1
 F32 = jnp.float32
 BF16 = jnp.bfloat16
 
@@ -418,8 +418,8 @@
     late = max(depth - 3, 0) * stride
     for group in groups:
         events += [
-            (0.9 + group[0], local_backward, (False, group)),
-            (4.9 + 0.5 * group[0], local_backward, (True, group)),
+            (0.9 + 0.2 * group[0], local_backward, (False, group)),
+            (2.3 + 0.2 * group[0], local_backward, (True, group)),
         ]
     for jj in range(parts):
         for b in range(2, depth):

time: 60.1 us -> 51.7 us (0.86)
  Pallas kernels: 59.2 us -> 50.9 us
    pallas_call x1, Pallas kernels: 57.1 us -> 48.7 us  [shards(): pl.pallas_call(functools.partial(kernel, ctx_count, head_count), out_shap...]
where the time goes in v5:
time: 51.7 us; the launch traced here: 51.5 us
  Pallas kernels  50.9 us (98%)
  between operations  0.64 us (1%)
    pallas_call x1, Pallas kernels, shards(): pl.pallas_call(functools.partial(kernel, ctx_count, head_count), out_shap...  48.7 us
    pallas_call x1, Pallas kernels, shards(): pl.pallas_call(land, out_shape=(block,) * 4, grid=(2,), in_specs=[rows] *...  2.13 us

profile of v5, /device:TPU:0, one launch (start us, length us, event | category | flops | bytes accessed | tf_op | source)
XLA Modules:
  0.0 51.5 jit_solution(6809560306538526974)
XLA Ops:
  0.6 48.7 %shard_map.111 = (bf16[128,1024]{1,0:T(8,128)(2,1)}, bf16[128,1024]{1,0:T(8,128)(2,1)}, bf16[128,1024]{1,0:T(8,128)(2,1)}, bf16[128,1024]{1,0:T(8,128)(2,1)}) custom-call(bf16[128,1024]{1,0:T(8,128)(2,1)} %q_hbm.1, bf16[128,1024]{1,0:T(8,128)(2,1)} %k_hbm.1, bf16[128,1024]{1,0:T(8,128)(2,1)} %v_hbm.1, bf16[128,1024]{1,0:T(8,128)(2,1)} %dy_hbm.1, ...), custom_call_target="tpu_custom_call" | custom-call | flops 603979776 | bytes 2097152 | tf_op jit(solution)/shard_map/pallas_call | solution.py:504
  49.4 2.1 %shard_map.112 = (bf16[128,1024]{1,0:T(8,128)(2,1)}, bf16[128,1024]{1,0:T(8,128)(2,1)}, bf16[128,1024]{1,0:T(8,128)(2,1)}, bf16[128,1024]{1,0:T(8,128)(2,1)}) custom-call(bf16[128,1024]{1,0:T(8,128)(2,1)} %get-tuple-element.8.refs_0_, bf16[128,1024]{1,0:T(8,128)(2,1)} %get-tuple-element.9.refs_1_, bf16[128,1024]{1,0:T(8,128)(2,1)} %get-tuple-element.10.refs_2_, ...), custom_call_target="tpu_custom_call" | custom-call | tf_op jit(solution)/shard_map/pallas_call | solution.py:565

commit v6 on v5

--- a/solution.py
+++ b/solution.py
@@ -34,10 +34,10 @@
     q_ref, k_ref, v_ref, dy_ref, kind_ref, table_ref, scale_ref, gain_ref,
     att_ref, gq_ref, gk_ref, gv_ref, kind_col, inv_col, coef_col,
     states, probs, query_t, readout, grad_out_ref, kind_sums, grad_states, key_acc, value_acc,
-    own_send, total_send, fwd_recv, half_send, half_recv, back_send, back_recv, last_send, last_recv,
+    own_send, total_send, fwd_recv, half_send, half_recv, back_send, back_recv, last_send, last_recv, late_send, late_recv,
     stat_send, stat_recv,
     load_sem, store_sem, own_ssem, total_ssem, relay_ssem, fwd_rsem, half_ssem, half_rsem,
-    back_ssem, back_rsem, last_ssem, last_rsem, stat_ssem, stat_rsem,
+    back_ssem, back_rsem, last_ssem, last_rsem, late_ssem, late_rsem, stat_ssem, stat_rsem,
 ):
     tokens, width = q_ref.shape
     heads, size, _ = states.shape
@@ -60,6 +60,9 @@
     place = [None] + [pair & ((1 << (b - 1)) - 1) for b in range(1, depth)]
     origin = [None] + [pair - place[b] - 1 for b in range(1, depth)]
     beside = {"ctx": c ^ 1}
+    if depth > 1:
+        late_gives = above[1]
+        late_takes = jnp.logical_and(source[1], pair + 1 != pairs - 1)
 
     def at_pair(other):
         return {"ctx": 2 * other + side}
@@ -96,6 +99,17 @@
             for t in range(1 << (b - 1)):
                 greet(at_pair(pair + 1 + t))
 
+        if b == 1:
+
+            @pl.when(late_gives)
+            def _():
+                greet({"ctx": (c - 2) ^ 1})
+
+            @pl.when(late_takes)
+            def _():
+                greet({"ctx": (c + 2) ^ 1})
+
+            greeted = greeted + jnp.where(jnp.logical_or(late_gives, late_takes), 1, 0)
         greeted = greeted + ((c >> b) & 1) + jnp.where(source[b], 1 << (b - 1), 0)
 
     def first_chunk(mine, jj):
@@ -147,6 +161,15 @@
     def last_copy(mine, jj):
         at, j = part(mine, jj), first_chunk(mine, jj)
         return remote(last_send.at[at], last_recv.at[at], last_ssem.at[j], last_rsem.at[j], beside)
+
+    def late_copy(across, jj):
+        at, j = part(True, jj), first_chunk(True, jj)
+        device = {"ctx": (c - 2) ^ 1} if across else {"ctx": c - 2}
+        return remote(late_send.at[at], late_recv.at[at], late_ssem.at[int(across), j], late_rsem.at[j], device)
+
+    def late_arrival(mine, jj):
+        at, j = part(mine, jj), first_chunk(mine, jj)
+        return remote(late_send.at[at], late_recv.at[at], late_ssem.at[0, j], late_rsem.at[j], beside)
 
     def takes(mine):
         return jnp.logical_or(odd, jnp.logical_and(inner, True if mine else source[1]))
@@ -311,7 +334,7 @@
 
     def send_bucket_grad(mine, jj):
         for h in chunk_heads(mine, jj):
-            back_send[1, h] = (grad_states[h] + message(1, h)).astype(BF16)
+            back_send[1, h] = message(1, h).astype(BF16)
         back_copy(1, mine, jj).start()
 
     for mine, group in [(mine, group) for mine in (False, True) for group in groups]:
@@ -340,7 +363,7 @@
 
         if depth > 1:
 
-            @pl.when(jnp.logical_and(upper[1], jnp.logical_not(above[1])) if mine else upper[1])
+            @pl.when(upper[1])
             def _():
                 for jj in group:
                     send_bucket_grad(mine, jj)
@@ -389,13 +412,23 @@
                 for h in chunk_heads(mine, jj):
                     grad_states[h] += back_recv[t, h].astype(F32)
 
-    def pass_bucket_grad(jj):
-        @pl.when(jnp.logical_and(upper[1], above[1]))
-        def _():
-            send_bucket_grad(True, jj)
-
-    def send_last(mine, jj):
-        @pl.when(takes(mine))
+    def send_late(jj):
+        @pl.when(late_gives)
+        def _():
+            for h in chunk_heads(True, jj):
+                late_send[h] = grad_states[h].astype(BF16)
+            for across in (True, False):
+                late_copy(across, jj).start()
+
+    def receive_late(mine, jj):
+        @pl.when(late_takes)
+        def _():
+            late_arrival(mine, jj).wait_recv()
+            for h in chunk_heads(mine, jj):
+                grad_states[h] += late_recv[h].astype(F32)
+
+    def send_last(mine, jj, when):
+        @pl.when(jnp.logical_and(takes(mine), when))
         def _():
             flag = side.astype(F32)
             for h in chunk_heads(mine, jj):
@@ -414,7 +447,10 @@
             gk_ref[:, cols(h)] = (key_acc[h] + dot(v_ref[:, cols(h)], state, NT)).astype(BF16)
             gv_ref[:, cols(h)] = (value_acc[h] + dot(k_ref[:, cols(h)], state, NN)).astype(BF16)
 
-    events = []
+    def store_queries():
+        stores[1].start()
+
+    events = [(2.49, store_queries, ())]
     late = max(depth - 3, 0) * stride
     for group in groups:
         events += [
@@ -430,19 +466,22 @@
             ]
         if depth > 1:
             events += [
-                (late + 3.4 + 2 * jj, pass_bucket_grad, (jj,)),
-                (late + 2.5 + jj, gather_grads, (1, False, jj)),
-                (late + 4.7 + 2 * jj, gather_grads, (1, True, jj)),
+                (late + 2.5 + 0.01 * jj, gather_grads, (1, False, jj)),
+                (late + 2.7 + 0.01 * jj, gather_grads, (1, True, jj)),
+                (late + 3.4 + 2 * jj, send_late, (jj,)),
+                (late + 3.5 + 2 * jj, send_last, (True, jj, late_gives)),
+                (late + 5.0 + 2 * jj, receive_late, (True, jj)),
+                (late + 5.2 + 2 * jj, receive_late, (False, jj)),
             ]
         events += [
-            (late + 2.6 + jj, send_last, (False, jj)),
-            (late + 4.8 + 2 * jj, send_last, (True, jj)),
-            (late + 5.0 + 2 * jj, finish, (True, jj)),
-            (late + 5.9 + 2 * jj, finish, (False, jj)),
+            (late + 2.6 + 0.01 * jj, send_last, (False, jj, True)),
+            (late + 2.8 + 0.01 * jj, send_last, (True, jj, jnp.logical_not(late_gives) if depth > 1 else True)),
+            (late + 5.1 + 2 * jj, finish, (True, jj)),
+            (late + 5.3 + 2 * jj, finish, (False, jj)),
         ]
     for _, event, at in sorted(events, key=lambda item: item[0]):
         event(*at)
-    for store in stores[1:]:
+    for store in stores[2:]:
         store.start()
 
     for copy in stat_copies:
@@ -452,6 +491,13 @@
         @pl.when(gives(mine))
         def _():
             own_copy(mine, jj).wait_send()
+
+        if mine and depth > 1:
+
+            @pl.when(late_gives)
+            def _():
+                for across in (True, False):
+                    late_copy(across, jj).wait_send()
 
         @pl.when(takes(mine))
         def _():
@@ -534,6 +580,8 @@
                 pltpu.VMEM((targets,) + square, BF16),
                 pltpu.VMEM(square, BF16),
                 pltpu.VMEM(square, BF16),
+                pltpu.VMEM(square, BF16),
+                pltpu.VMEM(square, BF16),
                 pltpu.VMEM((8, tokens), F32),
                 pltpu.VMEM((head_count - 1, 8, tokens), F32),
                 dma((8,)),
@@ -547,6 +595,8 @@
                 dma((depth, chunks)),
                 dma((targets, chunks)),
                 dma((chunks,)),
+                dma((chunks,)),
+                dma((2, chunks)),
                 dma((chunks,)),
                 dma((head_count - 1,)),
                 dma((head_count - 1,)),

time: 51.7 us -> 51.2 us (level)
  no operation moved by 1% of the time
where the time goes in v6:
time: 51.2 us; the launch traced here: 51.1 us
  Pallas kernels  50.4 us (98%)
  between operations  0.64 us (1%)
    pallas_call x1, Pallas kernels, shards(): pl.pallas_call(functools.partial(kernel, ctx_count, head_count), out_shap...  48.3 us
    pallas_call x1, Pallas kernels, shards(): pl.pallas_call(land, out_shape=(block,) * 4, grid=(2,), in_specs=[rows] *...  2.13 us

profile of v6, /device:TPU:0, one launch (start us, length us, event | category | flops | bytes accessed | tf_op | source)
XLA Modules:
  0.0 51.1 jit_solution(13201806097228250616)
XLA Ops:
  0.6 48.3 %shard_map.111 = (bf16[128,1024]{1,0:T(8,128)(2,1)}, bf16[128,1024]{1,0:T(8,128)(2,1)}, bf16[128,1024]{1,0:T(8,128)(2,1)}, bf16[128,1024]{1,0:T(8,128)(2,1)}) custom-call(bf16[128,1024]{1,0:T(8,128)(2,1)} %q_hbm.1, bf16[128,1024]{1,0:T(8,128)(2,1)} %k_hbm.1, bf16[128,1024]{1,0:T(8,128)(2,1)} %v_hbm.1, bf16[128,1024]{1,0:T(8,128)(2,1)} %dy_hbm.1, ...), custom_call_target="tpu_custom_call" | custom-call | flops 603979776 | bytes 2097152 | tf_op jit(solution)/shard_map/pallas_call | solution.py:550
  48.9 2.1 %shard_map.112 = (bf16[128,1024]{1,0:T(8,128)(2,1)}, bf16[128,1024]{1,0:T(8,128)(2,1)}, bf16[128,1024]{1,0:T(8,128)(2,1)}, bf16[128,1024]{1,0:T(8,128)(2,1)}) custom-call(bf16[128,1024]{1,0:T(8,128)(2,1)} %get-tuple-element.8.refs_0_, bf16[128,1024]{1,0:T(8,128)(2,1)} %get-tuple-element.9.refs_1_, bf16[128,1024]{1,0:T(8,128)(2,1)} %get-tuple-element.10.refs_2_, ...), custom_call_target="tpu_custom_call" | custom-call | tf_op jit(solution)/shard_map/pallas_call | solution.py:615

commit v7 on v6

--- a/solution.py
+++ b/solution.py
@@ -10,6 +10,7 @@
 EPSILON = 1e-06
 CHUNK = 4
 GROUP = 1
+AHEAD = 2
 F32 = jnp.float32
 BF16 = jnp.bfloat16
 
@@ -46,6 +47,7 @@
     pairs = ctx_count // 2
     half = heads // 2
     parts = half // CHUNK
+    ahead_parts = half // AHEAD
     c = lax.axis_index("ctx")
     me = lax.axis_index("head")
     pair, side = c >> 1, c & 1
@@ -112,14 +114,14 @@
             greeted = greeted + jnp.where(jnp.logical_or(late_gives, late_takes), 1, 0)
         greeted = greeted + ((c >> b) & 1) + jnp.where(source[b], 1 << (b - 1), 0)
 
-    def first_chunk(mine, jj):
-        return (side if mine else 1 - side) * parts + jj
-
-    def chunk_heads(mine, *several):
-        return [first_chunk(mine, jj) * CHUNK + i for jj in several for i in range(CHUNK)]
-
-    def part(mine, jj):
-        return pl.ds(first_chunk(mine, jj) * CHUNK, CHUNK)
+    def first_chunk(mine, jj, count=CHUNK):
+        return (side if mine else 1 - side) * (half // count) + jj
+
+    def chunk_heads(mine, *several, count=CHUNK):
+        return [first_chunk(mine, jj, count) * count + i for jj in several for i in range(count)]
+
+    def part(mine, jj, count=CHUNK):
+        return pl.ds(first_chunk(mine, jj, count) * count, count)
 
     def cols(h):
         return pl.ds(pl.multiple_of(h * size, size), size)
@@ -130,17 +132,17 @@
         )
 
     def own_copy(mine, jj):
-        at, j = part(mine, jj), first_chunk(mine, jj)
+        at, j = part(mine, jj, AHEAD), first_chunk(mine, jj, AHEAD)
         return remote(own_send.at[at], fwd_recv.at[0, at], own_ssem.at[j], fwd_rsem.at[0, j], beside)
 
     def total_copy(b, t, mine, jj):
-        at, j = part(mine, jj), first_chunk(mine, jj)
+        at, j = part(mine, jj, AHEAD), first_chunk(mine, jj, AHEAD)
         return remote(
             total_send.at[at], fwd_recv.at[b, at], total_ssem.at[t, j], fwd_rsem.at[b, j], at_pair(pair + 1 + t)
         )
 
     def relay_copy(b, mine, jj):
-        at, j = part(mine, jj), first_chunk(mine, jj)
+        at, j = part(mine, jj, AHEAD), first_chunk(mine, jj, AHEAD)
         return remote(fwd_recv.at[b, at], fwd_recv.at[b, at], relay_ssem.at[b, j], fwd_rsem.at[b, j], beside)
 
     def half_copy(b, mine, jj):
@@ -178,6 +180,7 @@
         return jnp.logical_or(side == 0, jnp.logical_and(inner, source[1] if mine else True))
 
     chunk_list = [(mine, jj) for mine in (False, True) for jj in range(parts)]
+    ahead_list = [(mine, jj) for mine in (False, True) for jj in range(ahead_parts)]
     groups = [tuple(range(jj, min(jj + GROUP, parts))) for jj in range(0, parts, GROUP)]
 
     def weight(kind, h, level):
@@ -196,8 +199,8 @@
 
     loads[0].wait()
     loads[1].wait()
-    for index, (mine, jj) in enumerate(chunk_list):
-        for h in chunk_heads(mine, jj):
+    for index, (mine, jj) in enumerate(ahead_list):
+        for h in chunk_heads(mine, jj, count=AHEAD):
             state = dot(k_ref[:, cols(h)], v_ref[:, cols(h)], TN)
             states[h] = state
             own_send[h] = state.astype(BF16)
@@ -224,7 +227,7 @@
             query_t[h] = jnp.transpose(q)
 
     def send_total(b, mine, jj):
-        for h in chunk_heads(mine, jj):
+        for h in chunk_heads(mine, jj, count=AHEAD):
             total_send[h] = states[h].astype(BF16)
         for t in reversed(range(1 << (b - 1))):
             total_copy(b, t, mine, jj).start()
@@ -237,7 +240,7 @@
                 readout[h] += token_weights(h, b + 1) * level
 
     def add_state(b, mine, jj):
-        for h in chunk_heads(mine, jj):
+        for h in chunk_heads(mine, jj, count=AHEAD):
             states[h] += fwd_recv[b, h].astype(F32)
 
     def receive_first(mine, jj):
@@ -270,20 +273,21 @@
                 send_total(b + 1, mine, jj)
 
     events = []
-    stride = 3 * parts + 5
+    stride = 3 * ahead_parts + 5
+    everything = tuple(range(parts))
     for mine in (True, False):
-        skip = 0 if mine else parts
-        for group in groups:
-            events += [
-                (0.5 + group[0] + skip, local_forward, (mine, group)),
-                (1.4 + group[-1] + skip, add_level, (0, mine, group)),
-            ]
-            if depth > 1:
-                events += [(2.7 + group[-1] + skip, add_level, (1, mine, group))]
-            for b in range(2, depth):
-                now = 4.6 + 2 * group[-1] + (b - 2) * stride + (0 if mine else 1.4)
-                events += [(now + 0.1, add_level, (b, mine, group))]
-        for jj in range(parts):
+        skip = 0 if mine else ahead_parts
+        done = 2 * ahead_parts
+        events += [
+            (0.5 if mine else 1.5, local_forward, (mine, everything)),
+            (1.4 + ahead_parts if mine else 1.5 + done, add_level, (0, mine, everything)),
+        ]
+        if depth > 1:
+            events += [((1.6 if mine else 1.7) + done, add_level, (1, mine, everything))]
+        for b in range(2, depth):
+            now = 4.6 + 2 * (ahead_parts - 1) + (b - 2) * stride + (0 if mine else 1.4)
+            events += [(now + 0.1, add_level, (b, mine, everything))]
+        for jj in range(ahead_parts):
             events += [(1.0 + jj + skip, receive_first, (mine, jj))]
             if depth > 1:
                 events += [(2.3 + jj + skip, receive_total, (1, mine, jj))]
@@ -486,22 +490,11 @@
 
     for copy in stat_copies:
         copy.wait_send()
-    for mine, jj in chunk_list:
+    for mine, jj in ahead_list:
 
         @pl.when(gives(mine))
         def _():
             own_copy(mine, jj).wait_send()
-
-        if mine and depth > 1:
-
-            @pl.when(late_gives)
-            def _():
-                for across in (True, False):
-                    late_copy(across, jj).wait_send()
-
-        @pl.when(takes(mine))
-        def _():
-            last_copy(mine, jj).wait_send()
 
         for b in range(1, depth):
             if mine or b == 1:
@@ -511,17 +504,30 @@
                     for t in range(1 << (b - 1)):
                         total_copy(b, t, mine, jj).wait_send()
 
+            if mine and b > 1:
+
                 @pl.when(upper[b])
                 def _():
-                    back_copy(b, mine, jj).wait_send()
-                    if b > 1:
-                        relay_copy(b, mine, jj).wait_send()
-
-            else:
-
-                @pl.when(upper[b])
-                def _():
-                    half_copy(b, mine, jj).wait_send()
+                    relay_copy(b, mine, jj).wait_send()
+
+    for mine, jj in chunk_list:
+        if mine and depth > 1:
+
+            @pl.when(late_gives)
+            def _():
+                for across in (True, False):
+                    late_copy(across, jj).wait_send()
+
+        @pl.when(takes(mine))
+        def _():
+            last_copy(mine, jj).wait_send()
+
+        for b in range(1, depth):
+            copy = back_copy if mine or b == 1 else half_copy
+
+            @pl.when(upper[b])
+            def _():
+                copy(b, mine, jj).wait_send()
 
     for store in stores:
         store.wait()
@@ -542,7 +548,7 @@
         tokens, width = queries.shape
         kinds, heads, _ = level_table.shape
         size = width // heads
-        chunks = heads // CHUNK
+        chunks = heads // min(CHUNK, AHEAD)
         hbm = pl.BlockSpec(memory_space=pltpu.HBM)
         block = jax.ShapeDtypeStruct((tokens, width), BF16)
         square = (heads, size, size)

time: 51.2 us -> 50.9 us (level)
  no operation moved by 1% of the time
where the time goes in v7:
time: 50.9 us; the launch traced here: 50.7 us
  Pallas kernels  50.1 us (98%)
  between operations  0.64 us (1%)
    pallas_call x1, Pallas kernels, shards(): pl.pallas_call(functools.partial(kernel, ctx_count, head_count), out_shap...  47.9 us
    pallas_call x1, Pallas kernels, shards(): pl.pallas_call(land, out_shape=(block,) * 4, grid=(2,), in_specs=[rows] *...  2.13 us

profile of v7, /device:TPU:0, one launch (start us, length us, event | category | flops | bytes accessed | tf_op | source)
XLA Modules:
  0.0 50.7 jit_solution(1770191795001103071)
XLA Ops:
  0.6 47.9 %shard_map.111 = (bf16[128,1024]{1,0:T(8,128)(2,1)}, bf16[128,1024]{1,0:T(8,128)(2,1)}, bf16[128,1024]{1,0:T(8,128)(2,1)}, bf16[128,1024]{1,0:T(8,128)(2,1)}) custom-call(bf16[128,1024]{1,0:T(8,128)(2,1)} %q_hbm.1, bf16[128,1024]{1,0:T(8,128)(2,1)} %k_hbm.1, bf16[128,1024]{1,0:T(8,128)(2,1)} %v_hbm.1, bf16[128,1024]{1,0:T(8,128)(2,1)} %dy_hbm.1, ...), custom_call_target="tpu_custom_call" | custom-call | flops 603979776 | bytes 2097152 | tf_op jit(solution)/shard_map/pallas_call | solution.py:556
  48.6 2.1 %shard_map.112 = (bf16[128,1024]{1,0:T(8,128)(2,1)}, bf16[128,1024]{1,0:T(8,128)(2,1)}, bf16[128,1024]{1,0:T(8,128)(2,1)}, bf16[128,1024]{1,0:T(8,128)(2,1)}) custom-call(bf16[128,1024]{1,0:T(8,128)(2,1)} %get-tuple-element.8.refs_0_, bf16[128,1024]{1,0:T(8,128)(2,1)} %get-tuple-element.9.refs_1_, bf16[128,1024]{1,0:T(8,128)(2,1)} %get-tuple-element.10.refs_2_, ...), custom_call_target="tpu_custom_call" | custom-call | tf_op jit(solution)/shard_map/pallas_call | solution.py:621
